TPU v7x, 256 devices: a whole 4x4x8 slice. The times are simulated.
256 devices in a mesh: dp: 64 (over z, y, core), heads: 4 (over x).
Axes of the slice: x: 4, y: 4, z: 8, core: 2. Of those that a mesh axis runs over, the one named last changes fastest.
Arguments:
- queries: bfloat16 [64, 128, 8192], P('dp', None, 'heads'), may hold values from -24 to 24
- query_gain: float32 [128], replicated, may hold values from 0.5 to 6
- image_key_rows: bfloat16 [128, 1601, 1024], P('dp', None, 'heads'), may hold values from -24 to 24
- image_value_rows: bfloat16 [128, 1601, 1024], P('dp', None, 'heads'), may hold values from -6 to 6
- key_gain: float32 [128], replicated, may hold values from 0.5 to 6
- gate_logit: float32 [1], replicated, may hold values from 0.3 to 1.5
- image_doc: int32 [128], replicated, may hold values from 0 to 63, as said below
- text_mask: int32 [64, 128, 5], replicated, may hold values from 0 to 1, as said below
- out_grad: bfloat16 [64, 128, 8192], P('dp', None, 'heads'), may hold values from -6 to 6
Outputs:
- attended: bfloat16 [64, 128, 8192], P('dp', None, 'heads')
- query_grad: bfloat16 [64, 128, 8192], P('dp', None, 'heads')
- image_key_gradient: bfloat16 [128, 1601, 1024], P('dp', None, 'heads')
- image_value_gradient: bfloat16 [128, 1601, 1024], P('dp', None, 'heads')
- query_gain_grad: float32 [128], replicated
- key_gain_grad: float32 [128], replicated
- gate_grad: float32 [1], replicated
Inputs may be any that keep to these rules, and one draw needn't show every extreme that they name: image_doc never falls; each aligned group of 4 documents holds 8 images, every document 1 to 5; in one group the first document has 5 images and the other three 1; where there are 12 documents or more, in another group the last has 5 and the other three 1. text_mask[d, t, k] is 1 when token t of document d sees the document's k-th image; the images of a document stand at rising token positions and a token sees those at or before it; columns from the document's image count on are 0.
All inputs are finite; a program needn't handle non-finite values.
Results may differ from a plain program's by a relative error of at most 0.0075.
The roundings to bfloat16 on the way count: a program that leaves them out, or rounds other values in their place, can miss the bound.
Values may be sent and summed in bfloat16 or wider, within the bound.
A program may use at most 192 MiB of HBM per device.

v0:
```python
import jax
import jax.numpy as jnp
from jax import lax
from jax.sharding import PartitionSpec as P

EPSILON = 1e-05
NEGATIVE = -1e30
OFFSETS = (-2, -1, 1, 2)


def from_behind(value, axis, by):
    length = lax.axis_size(axis)
    pairs = [(i, i + by) for i in range(length) if 0 <= i + by < length]
    return lax.ppermute(value, axis, pairs)


def normalized_rows(tensor):
    widened = tensor.astype(jnp.float32)
    inverse = lax.rsqrt(jnp.mean(widened * widened, axis=-1, keepdims=True) + EPSILON)
    return (widened * inverse, inverse)


def unit_back(upstream, normed, inverse, gain_row):
    scaled = upstream * gain_row
    result_grad = inverse * (scaled - normed * jnp.mean(scaled * normed, axis=-1, keepdims=True))
    return (result_grad, jnp.sum((upstream * normed).reshape(-1, normed.shape[-1]), axis=0))


def head_forward(query_block, key_one, value_one, seen_rows, score_scale):
    scores = (
        jnp.einsum("hld,cd->hlc", query_block, key_one, preferred_element_type=jnp.float32)
        * score_scale
    )
    row_max = jnp.max(scores, axis=-1, keepdims=True)
    log_total = row_max + jnp.log(jnp.sum(jnp.exp(scores - row_max), axis=-1, keepdims=True))
    soft_prob = jnp.exp(scores - log_total).astype(jnp.bfloat16)
    head_out = jnp.einsum("hlc,cd->hld", soft_prob, value_one, preferred_element_type=jnp.float32)
    head_out = jnp.where(seen_rows[None, :, None], head_out, 0.0)
    head_lse = jnp.where(seen_rows[None, :], log_total[..., 0], NEGATIVE)
    return (head_out, head_lse)


def head_backward(
    query_block, grad_block, lse_block, delta_block, key_one, value_one, seen_rows, score_scale
):
    scores = (
        jnp.einsum("hld,cd->hlc", query_block, key_one, preferred_element_type=jnp.float32)
        * score_scale
    )
    soft_prob = jnp.where(seen_rows[None, :, None], jnp.exp(scores - lse_block[..., None]), 0.0)
    value_part = jnp.einsum(
        "hlc,hld->cd",
        soft_prob.astype(jnp.bfloat16),
        grad_block,
        preferred_element_type=jnp.float32,
    )
    prob_grad = jnp.einsum("hld,cd->hlc", grad_block, value_one, preferred_element_type=jnp.float32)
    score_grad = (soft_prob * (prob_grad - delta_block[..., None])).astype(jnp.bfloat16)
    query_part = (
        jnp.einsum("hlc,cd->hld", score_grad, key_one, preferred_element_type=jnp.float32)
        * score_scale
    )
    key_part = (
        jnp.einsum("hlc,hld->cd", score_grad, query_block, preferred_element_type=jnp.float32)
        * score_scale
    )
    return (query_part, key_part, value_part)


def per_device(
    queries,
    query_gain,
    image_key_rows,
    image_value_rows,
    key_gain,
    gate_logit,
    image_doc,
    text_mask,
    out_grad,
):
    row_count = queries.shape[1]
    row_width = queries.shape[2]
    head_dim = query_gain.shape[0]
    query_heads = row_width // head_dim
    slot_count = image_key_rows.shape[0]
    image_len = image_key_rows.shape[1]
    key_heads = image_key_rows.shape[2] // head_dim
    heads_per_group = query_heads // key_heads
    owners = lax.axis_size("dp")
    my_index = lax.axis_index("dp")
    image_total = image_doc.shape[0]
    score_scale = head_dim ** (-0.5)
    image_ids = jnp.arange(image_total, dtype=jnp.int32)
    same_doc = image_doc[:, None] == image_doc[None, :]
    earlier = image_ids[None, :] < image_ids[:, None]
    image_rank = jnp.sum((same_doc & earlier).astype(jnp.int32), axis=1)
    slot_index = my_index * slot_count + jnp.arange(slot_count, dtype=jnp.int32)
    slot_doc = jnp.take(image_doc, slot_index)
    slot_rank = jnp.take(image_rank, slot_index)
    slot_mask = jnp.take(text_mask, slot_doc, axis=0)
    rank_hot = (
        slot_rank[:, None] == jnp.arange(text_mask.shape[2], dtype=jnp.int32)[None, :]
    ).astype(jnp.int32)
    slot_seen = jnp.sum(slot_mask * rank_hot[:, None, :], axis=2) > 0
    slot_shift = my_index - slot_doc

    def source_usable(offset, slot_number):
        holder = my_index + offset
        inside = (holder >= 0) & (holder < owners)
        image_slot = jnp.clip(holder * slot_count + slot_number, 0, image_total - 1)
        return inside & (jnp.take(image_doc, image_slot) == my_index)

    def select_rows(received, slot_number):
        result = received[0]
        for offset in OFFSETS:
            result = jnp.where(slot_shift[slot_number] == offset, received[offset], result)
        return result

    query_unit, query_inverse = normalized_rows(
        queries[0].reshape(row_count, query_heads, head_dim)
    )
    query_hat = (query_unit * query_gain).astype(jnp.bfloat16).reshape(row_count, row_width)
    gate_tanh = jnp.tanh(gate_logit[0])
    grad_scaled = (gate_tanh * out_grad[0].astype(jnp.float32)).astype(jnp.bfloat16)
    query_from = {0: query_hat}
    grad_from = {0: grad_scaled}
    for offset in OFFSETS:
        query_from[offset] = from_behind(query_hat, "dp", offset)
    key_unit_rows, key_inverse_norm = normalized_rows(
        image_key_rows.reshape(slot_count, image_len, key_heads, head_dim)
    )
    key_hat = (key_unit_rows * key_gain).astype(jnp.bfloat16)
    value_rows = image_value_rows.reshape(slot_count, image_len, key_heads, head_dim)
    slot_outs = []
    slot_lses = []
    for slot_number in range(slot_count):
        text_rows = select_rows(query_from, slot_number).reshape(
            row_count, key_heads, heads_per_group, head_dim
        )
        blocks = jnp.transpose(text_rows, (1, 2, 0, 3))
        head_outs = []
        head_lses = []
        for head_index in range(key_heads):
            out_block, lse_block = head_forward(
                blocks[head_index],
                key_hat[slot_number, :, head_index, :],
                value_rows[slot_number, :, head_index, :],
                slot_seen[slot_number],
                score_scale,
            )
            head_outs.append(out_block)
            head_lses.append(lse_block)
        out_stack = jnp.stack(head_outs, axis=0).reshape(query_heads, row_count, head_dim)
        lse_stack = jnp.stack(head_lses, axis=0).reshape(query_heads, row_count)
        slot_outs.append(jnp.transpose(out_stack, (1, 0, 2)).reshape(row_count, row_width))
        slot_lses.append(jnp.transpose(lse_stack, (1, 0)))
    send_out = jnp.stack(slot_outs, axis=0)
    send_lse = jnp.stack(slot_lses, axis=0)
    cand_outs = []
    cand_lses = []
    partial_from = {0: (send_out, send_lse)}
    for offset in OFFSETS:
        partial_from[offset] = from_behind((send_out, send_lse), "dp", -offset)
    for offset in (0,) + OFFSETS:
        arrived_out, arrived_lse = partial_from[offset]
        for slot_number in range(slot_count):
            usable = source_usable(offset, slot_number)
            cand_outs.append(jnp.where(usable, arrived_out[slot_number], 0.0))
            cand_lses.append(jnp.where(usable, arrived_lse[slot_number], 2.0 * NEGATIVE))
    cand_out = jnp.stack(cand_outs, axis=0).reshape(
        len(cand_outs), row_count, query_heads, head_dim
    )
    cand_lse = jnp.stack(cand_lses, axis=0)
    doc_max = jnp.max(cand_lse, axis=0)
    exp_terms = jnp.exp(cand_lse - doc_max[None])
    doc_total = jnp.sum(exp_terms, axis=0)
    doc_lse = doc_max + jnp.log(doc_total)
    weight = exp_terms / doc_total[None]
    merged = jnp.sum(weight[..., None] * cand_out, axis=0)
    attended = (gate_tanh * merged).astype(jnp.bfloat16).reshape(1, row_count, row_width)
    row_delta = jnp.sum(
        grad_scaled.reshape(row_count, query_heads, head_dim).astype(jnp.float32) * merged, axis=-1
    )
    gate_part = jnp.sum(
        out_grad[0].astype(jnp.float32).reshape(row_count, query_heads, head_dim) * merged
    )
    lse_from = {0: doc_lse}
    delta_from = {0: row_delta}
    for offset in OFFSETS:
        grad_wide, lse_from[offset], delta_from[offset] = from_behind(
            (grad_scaled.astype(jnp.float32), doc_lse, row_delta), "dp", offset
        )
        grad_from[offset] = grad_wide.astype(jnp.bfloat16)
    slot_queries = []
    key_slots = []
    value_slots = []
    for slot_number in range(slot_count):
        text_rows = select_rows(query_from, slot_number).reshape(
            row_count, key_heads, heads_per_group, head_dim
        )
        gradient_rows = select_rows(grad_from, slot_number).reshape(
            row_count, key_heads, heads_per_group, head_dim
        )
        logsumexp_rows = select_rows(lse_from, slot_number).reshape(
            row_count, key_heads, heads_per_group
        )
        delta_per_row = select_rows(delta_from, slot_number).reshape(
            row_count, key_heads, heads_per_group
        )
        query_blocks = jnp.transpose(text_rows, (1, 2, 0, 3))
        grad_blocks = jnp.transpose(gradient_rows, (1, 2, 0, 3))
        lse_blocks = jnp.transpose(logsumexp_rows, (1, 2, 0))
        delta_blocks = jnp.transpose(delta_per_row, (1, 2, 0))
        query_heads_list = []
        key_list = []
        value_list = []
        for head_index in range(key_heads):
            query_part, key_part, value_part = head_backward(
                query_blocks[head_index],
                grad_blocks[head_index],
                lse_blocks[head_index],
                delta_blocks[head_index],
                key_hat[slot_number, :, head_index, :],
                value_rows[slot_number, :, head_index, :],
                slot_seen[slot_number],
                score_scale,
            )
            query_heads_list.append(query_part)
            key_list.append(key_part)
            value_list.append(value_part)
        query_stack = jnp.stack(query_heads_list, axis=0).reshape(query_heads, row_count, head_dim)
        slot_queries.append(jnp.transpose(query_stack, (1, 0, 2)).reshape(row_count, row_width))
        key_slots.append(jnp.stack(key_list, axis=1))
        value_slots.append(jnp.stack(value_list, axis=1))
    send_query = jnp.stack(slot_queries, axis=0)
    key_hat_grad = jnp.stack(key_slots, axis=0)
    image_value_gradient = jnp.stack(value_slots, axis=0)
    hat_sum = jnp.zeros((row_count, row_width), jnp.float32)
    query_from_back = {0: send_query}
    for offset in OFFSETS:
        query_from_back[offset] = from_behind(send_query, "dp", -offset)
    for offset in (0,) + OFFSETS:
        for slot_number in range(slot_count):
            hat_sum = hat_sum + jnp.where(
                source_usable(offset, slot_number), query_from_back[offset][slot_number], 0.0
            )
    hat_grad = hat_sum.reshape(row_count, query_heads, head_dim)
    query_back, query_gain_part = unit_back(hat_grad, query_unit, query_inverse, query_gain)
    key_reverse_pass, key_gain_part = unit_back(
        key_hat_grad, key_unit_rows, key_inverse_norm, key_gain
    )
    query_gain_sum, key_gain_sum, gate_sum = lax.psum(
        (query_gain_part, key_gain_part, gate_part), ("dp", "heads")
    )
    gate_grad = ((1.0 - gate_tanh * gate_tanh) * gate_sum).reshape(1)
    query_grad = query_back.astype(jnp.bfloat16).reshape(1, row_count, row_width)
    image_key_gradient = key_reverse_pass.astype(jnp.bfloat16).reshape(
        slot_count, image_len, key_heads * head_dim
    )
    value_out = image_value_gradient.astype(jnp.bfloat16).reshape(
        slot_count, image_len, key_heads * head_dim
    )
    return (
        attended,
        query_grad,
        image_key_gradient,
        value_out,
        query_gain_sum,
        key_gain_sum,
        gate_grad,
    )


def solution(mesh):
    return jax.shard_map(
        per_device,
        mesh=mesh,
        in_specs=(
            P("dp", None, "heads"),
            P(),
            P("dp", None, "heads"),
            P("dp", None, "heads"),
            P(),
            P(),
            P(),
            P(),
            P("dp", None, "heads"),
        ),
        out_specs=(
            P("dp", None, "heads"),
            P("dp", None, "heads"),
            P("dp", None, "heads"),
            P("dp", None, "heads"),
            P(),
            P(),
            P(),
        ),
        check_vma=False,
    )
```

profile of v0, /device:TPU:1, one launch (start us, length us, event | category | flops | bytes accessed | tf_op | source)
XLA Modules:
  0.0 485.9 jit_solution(5627130652471833832)
XLA Ops:
  4.9 4.8 collective-permute-start
  9.8 3.2 collective-permute-start.1
  13.0 1.9 collective-permute-start.2
  25.0 1.7 fusion.148
  26.7 2.0 copy.52
  28.8 4.6 copy.44
  34.5 2.8 copy.45
  38.0 5.4 %copy.47 = bf16[2,1601,256]{1,2,0:T(8,128)(2,1)} copy(bf16[2,1601,256]{2,0,1:T(2,128)(2,1)} %param.14) | data formatting | bytes 3278848 | tf_op args[3]
  50.5 2.4 multiply_convert_fusion.4
  53.0 2.8 select_select_fusion
  55.8 2.0 copy.43
  57.8 4.9 %multiply_reduce_fusion.3 = (f32[8,128]{1,0:T(8,128)S(1)}, f32[8,128,1601]{1,2,0:T(8,128)}) fusion(bf16[2,1601,2,128]{3,1,2,0:T(8,128)(2,1)} %multiply_convert_fusion.4, bf16[2,8,128,128]{3,2,1,0:T(8,128)(2,1)} %bitcast.543), kind=kOutput, calls=%fused_computation.28 | convolution fusion | flops 422970368 | bytes 7235584 | tf_op jit(solution)/shard_map/hld,cd->hlc/dot_general | solution.py:31
  62.7 4.9 %multiply_reduce_fusion.4 = (f32[8,128]{1,0:T(8,128)S(1)}, f32[8,128,1601]{1,2,0:T(8,128)}) fusion(bf16[2,1601,2,128]{3,1,2,0:T(8,128)(2,1)} %multiply_convert_fusion.4, bf16[2,8,128,128]{3,2,1,0:T(8,128)(2,1)S(1)} %bitcast.544), kind=kOutput, calls=%fused_computation.29 | convolution fusion | flops 422970368 | bytes 7235584 | tf_op jit(solution)/shard_map/hld,cd->hlc/dot_general | solution.py:31
  67.6 2.0 copy.46
  69.6 2.3 multiply_reduce_fusion.1
  72.0 5.1 %multiply_reduce_fusion.2 = (f32[8,128]{1,0:T(8,128)S(1)}, f32[8,128,1601]{1,2,0:T(8,128)S(1)}) fusion(bf16[2,1601,2,128]{3,1,2,0:T(8,128)(2,1)} %multiply_convert_fusion.4, bf16[2,8,128,128]{3,2,1,0:T(8,128)(2,1)S(1)} %bitcast.548), kind=kOutput, calls=%fused_computation.27 | convolution fusion | flops 422970368 | bytes 7235584 | tf_op jit(solution)/shard_map/hld,cd->hlc/dot_general | solution.py:31
  87.8 4.1 collective-permute-start.8
  92.0 4.1 collective-permute-start.9
  96.0 1.9 collective-permute-start.10
  98.1 2.9 collective-permute-start.4
  101.0 3.9 collective-permute-start.5
  105.0 55.1 %collective-permute-done.4 = f32[2,128,16]{1,2,0:T(8,128)S(1)} collective-permute-done((f32[2,128,16]{1,2,0:T(8,128)S(1)}, f32[2,128,16]{1,2,0:T(8,128)S(1)}, u32[]{:S(2)}, u32[]{:S(2)}) %collective-permute-start.4) | collective-permute-done | bytes 16416 | tf_op jit(solution)/shard_map/ppermute | solution.py:14
  160.1 1.9 collective-permute-start.6
  163.4 1.8 collective-permute-done.6
  165.2 2.4 collective-permute-done.7
  167.7 2.9 collective-permute-start.12
  170.6 5.2 %collective-permute-start.13 = (f32[128,16]{0,1:T(8,128)S(1)}, f32[128,16]{0,1:T(8,128)S(1)}, u32[]{:S(2)}, u32[]{:S(2)}) collective-permute-start(f32[128,16]{0,1:T(8,128)S(1)} %fusion.120), channel_id=1, source_target_pairs={{0,4},{4,8},{8,12},{12,16},{16,20},{20,24},{24,28},{28,32},{32,36}... | collective-permute-start | bytes 24584 | tf_op jit(solution)/shard_map/ppermute | solution.py:14
  175.8 1.9 collective-permute-start.14
  179.1 1.7 collective-permute-done.14
  182.1 2.8 collective-permute-done.15
  185.9 45.1 %collective-permute-done.11 = f32[2,128,2048]{1,2,0:T(8,128)S(1)} collective-permute-done((f32[2,128,2048]{1,2,0:T(8,128)S(1)}, f32[2,128,2048]{1,2,0:T(8,128)S(1)}, u32[]{:S(2)}, u32[]{:S(2)}) %collective-permute-start.11) | collective-permute-done | bytes 2097184 | tf_op jit(solution)/shard_map/ppermute | solution.py:14
  231.4 1.8 multiply_reduce_fusion
  233.2 1.7 fusion.89
  235.7 4.6 collective-permute-start.20
  240.3 1.9 collective-permute-start.21
  242.2 2.4 collective-permute-start.22
  246.0 2.0 copy.61
  249.3 1.9 collective-permute-start.18
  251.2 4.9 %collective-permute-start.17 = (bf16[128,2048]{0,1:T(8,128)(2,1)}, bf16[128,2048]{0,1:T(8,128)(2,1)S(1)}, u32[]{:S(2)}, u32[]{:S(2)}) collective-permute-start(bf16[128,2048]{0,1:T(8,128)(2,1)} %bitcast.522), channel_id=1, source_target_pairs={{0,4},{4,8},{8,12},{12,16},{16,20},{20,24},{24,28},{28,32},{32,36}... | collective-permute-start | bytes 1572872 | tf_op jit(solution)/shard_map/ppermute | solution.py:14
  256.2 6.0 %collective-permute-start.16 = (bf16[128,2048]{0,1:T(8,128)(2,1)}, bf16[128,2048]{0,1:T(8,128)(2,1)S(1)}, u32[]{:S(2)}, u32[]{:S(2)}) collective-permute-start(bf16[128,2048]{0,1:T(8,128)(2,1)} %bitcast.523), channel_id=1, source_target_pairs={{0,8},{4,12},{8,16},{12,20},{16,24},{20,28},{24,32},{28,36},{32,40... | collective-permute-start | bytes 1572872 | tf_op jit(solution)/shard_map/ppermute | solution.py:14
  262.2 4.1 collective-permute-done.19
  266.4 4.2 collective-permute-done.18
  270.6 3.2 collective-permute-done.16
  273.8 2.2 fusion.105
  276.0 2.0 copy.54
  278.0 5.3 %multiply_convert_fusion = bf16[8,128,1601]{1,2,0:T(8,128)(2,1)S(1)} fusion(f32[8,128,1601]{1,2,0:T(8,128)} %copy-done.6, f32[8,128]{1,0:T(8,128)S(1)} %get-tuple-element.190, f32[8,128]{1,0:T(8,128)S(1)} %get-tuple-element.188, pred[128]{0:T(512)(128)(4,1)S(1)} %get-tuple-element.203, bf16[2,1601,2,128]{1,3,2,0:T(8,128)(2,1)} %bitcast.556, ...), kind=kOutput, calls=%fused_computation.4 | convolution fusion | flops 429529088 | bytes 10561664 | tf_op jit(solution)/shard_map/hld,cd->hlc/dot_general | solution.py:57
  283.3 1.9 fusion.79
  285.3 5.0 %multiply_convert_fusion.1 = bf16[8,128,1601]{1,2,0:T(8,128)(2,1)S(1)} fusion(f32[8,128,1601]{1,2,0:T(8,128)} %copy-done.5, f32[8,128]{1,0:T(8,128)S(1)} %get-tuple-element.189, f32[8,128]{1,0:T(8,128)S(1)} %get-tuple-element.187, pred[128]{0:T(512)(128)(4,1)S(1)} %get-tuple-element.203, bf16[2,1601,2,128]{1,3,2,0:T(8,128)(2,1)} %bitcast.557, ...), kind=kOutput, calls=%fused_computation.6 | convolution fusion | flops 429529088 | bytes 10562048 | tf_op jit(solution)/shard_map/hld,cd->hlc/dot_general | solution.py:57
  290.3 1.9 fusion.78
  292.2 2.0 copy.53
  294.3 5.3 %multiply_convert_fusion.2 = bf16[8,128,1601]{1,2,0:T(8,128)(2,1)S(1)} fusion(f32[8,128,1601]{1,2,0:T(8,128)} %get-tuple-element.212, f32[8,128]{1,0:T(8,128)S(1)} %get-tuple-element.186, f32[8,128]{1,0:T(8,128)S(1)} %get-tuple-element.184, pred[128]{0:T(512)(128)(4,1)S(1)} %get-tuple-element.204, bf16[2,1601,2,128]{1,3,2,0:T(8,128)(2,1)} %bitcast.558, ...), kind=kOutput, calls=%fused_computation.8 | convolution fusion | flops 429529088 | bytes 10561664 | tf_op jit(solution)/shard_map/hld,cd->hlc/dot_general | solution.py:57
  300.3 5.1 %multiply_convert_fusion.3 = bf16[8,128,1601]{1,2,0:T(8,128)(2,1)S(1)} fusion(f32[8,128,1601]{1,2,0:T(8,128)} %get-tuple-element.210, f32[8,128]{1,0:T(8,128)S(1)} %get-tuple-element.185, f32[8,128]{1,0:T(8,128)S(1)} %get-tuple-element.183, pred[128]{0:T(512)(128)(4,1)S(1)} %get-tuple-element.204, bf16[2,1601,2,128]{1,3,2,0:T(8,128)(2,1)} %bitcast.559, ...), kind=kOutput, calls=%fused_computation.10 | convolution fusion | flops 429529088 | bytes 10562048 | tf_op jit(solution)/shard_map/hld,cd->hlc/dot_general | solution.py:57
  309.4 1.9 collective-permute-start.26
  311.4 5.4 %collective-permute-start.25 = (f32[2,128,2048]{1,2,0:T(8,128)}, f32[2,128,2048]{1,2,0:T(8,128)}, u32[]{:S(2)}, u32[]{:S(2)}) collective-permute-start(f32[2,128,2048]{1,2,0:T(8,128)} %pad_maximum_fusion.2), channel_id=1, source_target_pairs={{0,4},{4,8},{8,12},{12,16},{16,20},{20,24},{24,28},{28,32},{32,36}... | collective-permute-start | bytes 6291464 | tf_op jit(solution)/shard_map/ppermute | solution.py:14
  316.8 6.4 %collective-permute-start.24 = (f32[2,128,2048]{1,2,0:T(8,128)}, f32[2,128,2048]{1,2,0:T(8,128)}, u32[]{:S(2)}, u32[]{:S(2)}) collective-permute-start(f32[2,128,2048]{1,2,0:T(8,128)} %pad_maximum_fusion.2), channel_id=1, source_target_pairs={{0,8},{4,12},{8,16},{12,20},{16,24},{20,28},{24,32},{28,36},{32,40... | collective-permute-start | bytes 6291464 | tf_op jit(solution)/shard_map/ppermute | solution.py:14
  333.7 2.2 fusion.11
  340.9 1.8 copy.58
  342.7 2.7 copy.57
  345.4 3.9 multiply_reduce_fusion.5
  349.3 5.4 %copy.62 = bf16[2,1601,256]{2,0,1:T(2,128)(2,1)} copy(bf16[2,1601,256]{1,2,0:T(8,128)(2,1)} %get-tuple-element.151) | data formatting | bytes 3278848
  357.9 3.5 copy.63
  363.2 18.7 %collective-permute-done.26 = f32[2,128,2048]{1,2,0:T(8,128)} collective-permute-done((f32[2,128,2048]{1,2,0:T(8,128)}, f32[2,128,2048]{1,2,0:T(8,128)}, u32[]{:S(2)}, u32[]{:S(2)}) %collective-permute-start.26) | collective-permute-done | bytes 2097184 | tf_op jit(solution)/shard_map/ppermute | solution.py:14
  383.6 1.7 slice_select_fusion.5
  389.9 94.0 %all-reduce = (f32[128]{0:T(128)}, f32[128]{0:T(128)}, f32[]{:T(128)}) all-reduce(f32[128]{0:T(128)S(1)} %get-tuple-element.132, f32[128]{0:T(128)S(1)} %bitcast_reduce_fusion, f32[]{:T(128)} %get-tuple-element.176), channel_id=1, replica_groups=mesh['dp'=64,'heads'=4] {'dp','heads'}, use_global_device_ids=true, to_apply=%region_18.20 | all-reduce | flops 257 | bytes 2056 | tf_op jit(solution)/shard_map/psum | solution.py:252
  (216 shorter events, 61.8 us)
Async XLA Ops:
  0.6 36.7 %copy-start = (s32[64,128,5]{1,0,2:T(8,128)S(1)}, s32[64,128,5]{1,0,2:T(8,128)}, u32[]{:S(2)}) copy-start(s32[64,128,5]{1,0,2:T(8,128)} %param.18) | copy-start | bytes 491524
  4.9 48.0 %collective-permute-start = (bf16[128,2048]{0,1:T(8,128)(2,1)}, bf16[128,2048]{0,1:T(8,128)(2,1)}, u32[]{:S(2)}, u32[]{:S(2)}) collective-permute-start(bf16[128,2048]{0,1:T(8,128)(2,1)} %fusion.102), channel_id=1, source_target_pairs={{0,8},{4,12},{8,16},{12,20},{16,24},{20,28},{24,32},{28,36},{32,40... | collective-permute-start | bytes 1572872 | tf_op jit(solution)/shard_map/ppermute | solution.py:14
  9.8 43.2 %collective-permute-start.1 = (bf16[128,2048]{0,1:T(8,128)(2,1)}, bf16[128,2048]{0,1:T(8,128)(2,1)}, u32[]{:S(2)}, u32[]{:S(2)}) collective-permute-start(bf16[128,2048]{0,1:T(8,128)(2,1)} %fusion.102), channel_id=1, source_target_pairs={{0,4},{4,8},{8,12},{12,16},{16,20},{20,24},{24,28},{28,32},{32,36}... | collective-permute-start | bytes 1572872 | tf_op jit(solution)/shard_map/ppermute | solution.py:14
  13.0 39.9 %collective-permute-start.2 = (bf16[128,2048]{0,1:T(8,128)(2,1)}, bf16[128,2048]{0,1:T(8,128)(2,1)}, u32[]{:S(2)}, u32[]{:S(2)}) collective-permute-start(bf16[128,2048]{0,1:T(8,128)(2,1)} %fusion.102), channel_id=1, source_target_pairs={{4,0},{8,4},{12,8},{16,12},{20,16},{24,20},{28,24},{32,28},{36,32}... | collective-permute-start | bytes 1572872 | tf_op jit(solution)/shard_map/ppermute | solution.py:14
  15.0 38.0 %collective-permute-start.3 = (bf16[128,2048]{0,1:T(8,128)(2,1)}, bf16[128,2048]{0,1:T(8,128)(2,1)}, u32[]{:S(2)}, u32[]{:S(2)}) collective-permute-start(bf16[128,2048]{0,1:T(8,128)(2,1)} %fusion.102), channel_id=1, source_target_pairs={{8,0},{12,4},{16,8},{20,12},{24,16},{28,20},{32,24},{36,28},{40,32... | collective-permute-start | bytes 1572872 | tf_op jit(solution)/shard_map/ppermute | solution.py:14
  28.8 21.7 %copy-start.27 = (f32[128]{0:T(128)S(1)}, f32[128]{0:T(128)}, u32[]{:S(2)}) copy-start(f32[128]{0:T(128)} %param.15) | copy-start | bytes 1540
  57.8 4.9 %copy-start.15 = (bf16[128,2,8,128]{3,0,2,1:T(8,128)(2,1)S(1)}, bf16[128,2,8,128]{3,0,2,1:T(8,128)(2,1)}, u32[]{:S(2)}) copy-start(bf16[128,2,8,128]{3,0,2,1:T(8,128)(2,1)} %copy.43) | copy-start | bytes 1572868
  69.6 2.3 copy-start.18
  69.6 7.4 %copy-start.4 = (f32[8,128,1601]{1,2,0:T(8,128)S(1)}, f32[8,128,1601]{1,2,0:T(8,128)}, u32[]{:S(2)}) copy-start(f32[8,128,1601]{1,2,0:T(8,128)} %get-tuple-element.210) | copy-start | bytes 19673092
  69.6 8.5 %slice-start.2 = ((s8[6586368]{0:T(1024)(128)(4,1)}), s8[4194304]{0:T(1024)(128)(4,1)S(1)}, s32[]{:S(2)}) async-start(s8[6586368]{0:T(1024)(128)(4,1)} %bitcast.505), calls=%async_computation.2 | async-start | bytes 8388608
  71.9 12.8 %copy-start.6 = (f32[8,128,1601]{1,2,0:T(8,128)}, f32[8,128,1601]{1,2,0:T(8,128)S(1)}, u32[]{:S(2)}) copy-start(f32[8,128,1601]{1,2,0:T(8,128)S(1)} %get-tuple-element.216) | copy-start | bytes 19673092
  72.0 6.2 %slice-start.3 = ((s8[6586368]{0:T(1024)(128)(4,1)}), s8[2392064]{0:T(1024)(128)(4,1)S(1)}, s32[]{:S(2)}) async-start(s8[6586368]{0:T(1024)(128)(4,1)} %bitcast.505), calls=%async_computation.3 | async-start | bytes 4784128
  77.1 9.1 %copy-start.5 = (f32[8,128,1601]{1,2,0:T(8,128)}, f32[8,128,1601]{1,2,0:T(8,128)S(1)}, u32[]{:S(2)}) copy-start(f32[8,128,1601]{1,2,0:T(8,128)S(1)} %get-tuple-element.214) | copy-start | bytes 19673092
  77.1 2.8 copy-start.20
  87.8 97.0 %collective-permute-start.8 = (f32[2,128,2048]{1,2,0:T(8,128)S(1)}, f32[2,128,2048]{1,2,0:T(8,128)S(1)}, u32[]{:S(2)}, u32[]{:S(2)}) collective-permute-start(f32[2,128,2048]{1,2,0:T(8,128)S(1)} %pad_maximum_fusion.1), channel_id=1, source_target_pairs={{0,8},{4,12},{8,16},{12,20},{16,24},{20,28},{24,32},{28,36},{32,40... | collective-permute-start | bytes 6291464 | tf_op jit(solution)/shard_map/ppermute | solution.py:14
  92.0 93.2 %collective-permute-start.9 = (f32[2,128,2048]{1,2,0:T(8,128)S(1)}, f32[2,128,2048]{1,2,0:T(8,128)S(1)}, u32[]{:S(2)}, u32[]{:S(2)}) collective-permute-start(f32[2,128,2048]{1,2,0:T(8,128)S(1)} %pad_maximum_fusion.1), channel_id=1, source_target_pairs={{0,4},{4,8},{8,12},{12,16},{16,20},{20,24},{24,28},{28,32},{32,36}... | collective-permute-start | bytes 6291464 | tf_op jit(solution)/shard_map/ppermute | solution.py:14
  96.0 89.5 %collective-permute-start.10 = (f32[2,128,2048]{1,2,0:T(8,128)S(1)}, f32[2,128,2048]{1,2,0:T(8,128)S(1)}, u32[]{:S(2)}, u32[]{:S(2)}) collective-permute-start(f32[2,128,2048]{1,2,0:T(8,128)S(1)} %pad_maximum_fusion.1), channel_id=1, source_target_pairs={{4,0},{8,4},{12,8},{16,12},{20,16},{24,20},{28,24},{32,28},{36,32}... | collective-permute-start | bytes 6291464 | tf_op jit(solution)/shard_map/ppermute | solution.py:14
  98.1 62.0 %collective-permute-start.4 = (f32[2,128,16]{1,2,0:T(8,128)S(1)}, f32[2,128,16]{1,2,0:T(8,128)S(1)}, u32[]{:S(2)}, u32[]{:S(2)}) collective-permute-start(f32[2,128,16]{1,2,0:T(8,128)S(1)} %pad_maximum_fusion.12), channel_id=1, source_target_pairs={{0,8},{4,12},{8,16},{12,20},{16,24},{20,28},{24,32},{28,36},{32,40... | collective-permute-start | bytes 49160 | tf_op jit(solution)/shard_map/ppermute | solution.py:14
  101.0 61.0 %collective-permute-start.5 = (f32[2,128,16]{1,2,0:T(8,128)S(1)}, f32[2,128,16]{1,2,0:T(8,128)S(1)}, u32[]{:S(2)}, u32[]{:S(2)}) collective-permute-start(f32[2,128,16]{1,2,0:T(8,128)S(1)} %pad_maximum_fusion.12), channel_id=1, source_target_pairs={{0,4},{4,8},{8,12},{12,16},{16,20},{20,24},{24,28},{28,32},{32,36}... | collective-permute-start | bytes 49160 | tf_op jit(solution)/shard_map/ppermute | solution.py:14
  160.1 5.0 %collective-permute-start.6 = (f32[2,128,16]{1,2,0:T(8,128)S(1)}, f32[2,128,16]{1,2,0:T(8,128)S(1)}, u32[]{:S(2)}, u32[]{:S(2)}) collective-permute-start(f32[2,128,16]{1,2,0:T(8,128)S(1)} %pad_maximum_fusion.12), channel_id=1, source_target_pairs={{4,0},{8,4},{12,8},{16,12},{20,16},{24,20},{28,24},{32,28},{36,32}... | collective-permute-start | bytes 49160 | tf_op jit(solution)/shard_map/ppermute | solution.py:14
  162.0 5.5 %collective-permute-start.7 = (f32[2,128,16]{1,2,0:T(8,128)S(1)}, f32[2,128,16]{1,2,0:T(8,128)S(1)}, u32[]{:S(2)}, u32[]{:S(2)}) collective-permute-start(f32[2,128,16]{1,2,0:T(8,128)S(1)} %pad_maximum_fusion.12), channel_id=1, source_target_pairs={{8,0},{12,4},{16,8},{20,12},{24,16},{28,20},{32,24},{36,28},{40,32... | collective-permute-start | bytes 49160 | tf_op jit(solution)/shard_map/ppermute | solution.py:14
  167.7 8.2 %collective-permute-start.12 = (f32[128,16]{0,1:T(8,128)S(1)}, f32[128,16]{0,1:T(8,128)S(1)}, u32[]{:S(2)}, u32[]{:S(2)}) collective-permute-start(f32[128,16]{0,1:T(8,128)S(1)} %fusion.120), channel_id=1, source_target_pairs={{0,8},{4,12},{8,16},{12,20},{16,24},{20,28},{24,32},{28,36},{32,40... | collective-permute-start | bytes 24584 | tf_op jit(solution)/shard_map/ppermute | solution.py:14
  170.6 7.2 %collective-permute-start.13 = (f32[128,16]{0,1:T(8,128)S(1)}, f32[128,16]{0,1:T(8,128)S(1)}, u32[]{:S(2)}, u32[]{:S(2)}) collective-permute-start(f32[128,16]{0,1:T(8,128)S(1)} %fusion.120), channel_id=1, source_target_pairs={{0,4},{4,8},{8,12},{12,16},{16,20},{20,24},{24,28},{28,32},{32,36}... | collective-permute-start | bytes 24584 | tf_op jit(solution)/shard_map/ppermute | solution.py:14
  175.8 5.0 %collective-permute-start.14 = (f32[128,16]{0,1:T(8,128)S(1)}, f32[128,16]{0,1:T(8,128)S(1)}, u32[]{:S(2)}, u32[]{:S(2)}) collective-permute-start(f32[128,16]{0,1:T(8,128)S(1)} %fusion.120), channel_id=1, source_target_pairs={{4,0},{8,4},{12,8},{16,12},{20,16},{24,20},{28,24},{32,28},{36,32}... | collective-permute-start | bytes 24584 | tf_op jit(solution)/shard_map/ppermute | solution.py:14
  177.8 7.1 %collective-permute-start.15 = (f32[128,16]{0,1:T(8,128)S(1)}, f32[128,16]{0,1:T(8,128)S(1)}, u32[]{:S(2)}, u32[]{:S(2)}) collective-permute-start(f32[128,16]{0,1:T(8,128)S(1)} %fusion.120), channel_id=1, source_target_pairs={{8,0},{12,4},{16,8},{20,12},{24,16},{28,20},{32,24},{36,28},{40,32... | collective-permute-start | bytes 24584 | tf_op jit(solution)/shard_map/ppermute | solution.py:14
  180.8 50.2 %collective-permute-start.11 = (f32[2,128,2048]{1,2,0:T(8,128)S(1)}, f32[2,128,2048]{1,2,0:T(8,128)S(1)}, u32[]{:S(2)}, u32[]{:S(2)}) collective-permute-start(f32[2,128,2048]{1,2,0:T(8,128)S(1)} %pad_maximum_fusion.1), channel_id=1, source_target_pairs={{8,0},{12,4},{16,8},{20,12},{24,16},{28,20},{32,24},{36,28},{40,32... | collective-permute-start | bytes 6291464 | tf_op jit(solution)/shard_map/ppermute | solution.py:14
  235.7 13.6 %collective-permute-start.20 = (f32[128,16]{0,1:T(8,128)S(1)}, f32[128,16]{0,1:T(8,128)S(1)}, u32[]{:S(2)}, u32[]{:S(2)}) collective-permute-start(f32[128,16]{0,1:T(8,128)S(1)} %fusion.90), channel_id=1, source_target_pairs={{0,8},{4,12},{8,16},{12,20},{16,24},{20,28},{24,32},{28,36},{32,40... | collective-permute-start | bytes 24584 | tf_op jit(solution)/shard_map/ppermute | solution.py:14
  240.3 10.9 %collective-permute-start.21 = (f32[128,16]{0,1:T(8,128)S(1)}, f32[128,16]{0,1:T(8,128)S(1)}, u32[]{:S(2)}, u32[]{:S(2)}) collective-permute-start(f32[128,16]{0,1:T(8,128)S(1)} %fusion.90), channel_id=1, source_target_pairs={{0,4},{4,8},{8,12},{12,16},{16,20},{20,24},{24,28},{28,32},{32,36}... | collective-permute-start | bytes 24584 | tf_op jit(solution)/shard_map/ppermute | solution.py:14
  242.2 13.9 %collective-permute-start.22 = (f32[128,16]{0,1:T(8,128)S(1)}, f32[128,16]{0,1:T(8,128)S(1)}, u32[]{:S(2)}, u32[]{:S(2)}) collective-permute-start(f32[128,16]{0,1:T(8,128)S(1)} %fusion.90), channel_id=1, source_target_pairs={{4,0},{8,4},{12,8},{16,12},{20,16},{24,20},{28,24},{32,28},{36,32}... | collective-permute-start | bytes 24584 | tf_op jit(solution)/shard_map/ppermute | solution.py:14
  244.7 17.5 %collective-permute-start.23 = (f32[128,16]{0,1:T(8,128)S(1)}, f32[128,16]{0,1:T(8,128)S(1)}, u32[]{:S(2)}, u32[]{:S(2)}) collective-permute-start(f32[128,16]{0,1:T(8,128)S(1)} %fusion.90), channel_id=1, source_target_pairs={{8,0},{12,4},{16,8},{20,12},{24,16},{28,20},{32,24},{36,28},{40,32... | collective-permute-start | bytes 24584 | tf_op jit(solution)/shard_map/ppermute | solution.py:14
  248.0 18.4 %collective-permute-start.19 = (bf16[128,2048]{0,1:T(8,128)(2,1)}, bf16[128,2048]{0,1:T(8,128)(2,1)S(1)}, u32[]{:S(2)}, u32[]{:S(2)}) collective-permute-start(bf16[128,2048]{0,1:T(8,128)(2,1)} %bitcast.520), channel_id=1, source_target_pairs={{8,0},{12,4},{16,8},{20,12},{24,16},{28,20},{32,24},{36,28},{40,32... | collective-permute-start | bytes 1572872 | tf_op jit(solution)/shard_map/ppermute | solution.py:14
  249.3 21.3 %collective-permute-start.18 = (bf16[128,2048]{0,1:T(8,128)(2,1)}, bf16[128,2048]{0,1:T(8,128)(2,1)S(1)}, u32[]{:S(2)}, u32[]{:S(2)}) collective-permute-start(bf16[128,2048]{0,1:T(8,128)(2,1)} %bitcast.521), channel_id=1, source_target_pairs={{4,0},{8,4},{12,8},{16,12},{20,16},{24,20},{28,24},{32,28},{36,32}... | collective-permute-start | bytes 1572872 | tf_op jit(solution)/shard_map/ppermute | solution.py:14
  251.2 19.4 %collective-permute-start.17 = (bf16[128,2048]{0,1:T(8,128)(2,1)}, bf16[128,2048]{0,1:T(8,128)(2,1)S(1)}, u32[]{:S(2)}, u32[]{:S(2)}) collective-permute-start(bf16[128,2048]{0,1:T(8,128)(2,1)} %bitcast.522), channel_id=1, source_target_pairs={{0,4},{4,8},{8,12},{12,16},{16,20},{20,24},{24,28},{28,32},{32,36}... | collective-permute-start | bytes 1572872 | tf_op jit(solution)/shard_map/ppermute | solution.py:14
  256.2 17.6 %collective-permute-start.16 = (bf16[128,2048]{0,1:T(8,128)(2,1)}, bf16[128,2048]{0,1:T(8,128)(2,1)S(1)}, u32[]{:S(2)}, u32[]{:S(2)}) collective-permute-start(bf16[128,2048]{0,1:T(8,128)(2,1)} %bitcast.523), channel_id=1, source_target_pairs={{0,8},{4,12},{8,16},{12,20},{16,24},{20,28},{24,32},{28,36},{32,40... | collective-permute-start | bytes 1572872 | tf_op jit(solution)/shard_map/ppermute | solution.py:14
  278.0 5.3 %copy-start.12 = (bf16[2,1601,2,128]{3,1,2,0:T(8,128)(2,1)S(1)}, bf16[2,1601,2,128]{3,1,2,0:T(8,128)(2,1)}, u32[]{:S(2)}) copy-start(bf16[2,1601,2,128]{3,1,2,0:T(8,128)(2,1)} %multiply_convert_fusion.4) | copy-start | bytes 4918276
  278.0 7.2 %copy-start.22 = (bf16[128,2,8,128]{3,0,2,1:T(8,128)(2,1)S(1)}, bf16[128,2,8,128]{3,0,2,1:T(8,128)(2,1)}, u32[]{:S(2)}) copy-start(bf16[128,2,8,128]{3,0,2,1:T(8,128)(2,1)} %copy.54) | copy-start | bytes 1572868
  283.3 7.0 %copy-start.28 = (bf16[8,128,1601]{1,2,0:T(8,128)(2,1)}, bf16[8,128,1601]{1,2,0:T(8,128)(2,1)S(1)}, u32[]{:S(2)}) copy-start(bf16[8,128,1601]{1,2,0:T(8,128)(2,1)S(1)} %multiply_convert_fusion) | copy-start | bytes 9836548
  294.2 5.3 %copy-start.13 = (bf16[2,1601,2,128]{3,1,2,0:T(8,128)(2,1)S(1)}, bf16[2,1601,2,128]{3,1,2,0:T(8,128)(2,1)}, u32[]{:S(2)}) copy-start(bf16[2,1601,2,128]{3,1,2,0:T(8,128)(2,1)} %multiply_convert_fusion.4) | copy-start | bytes 4918276
  294.2 6.0 %copy-start.21 = (bf16[128,2,8,128]{3,0,2,1:T(8,128)(2,1)S(1)}, bf16[128,2,8,128]{3,0,2,1:T(8,128)(2,1)}, u32[]{:S(2)}) copy-start(bf16[128,2,8,128]{3,0,2,1:T(8,128)(2,1)} %copy.53) | copy-start | bytes 1572868
  300.3 5.9 %copy-start.24 = (f32[1,8,128,128]{2,3,1,0:T(8,128)S(1)}, f32[1,8,128,128]{2,3,1,0:T(8,128)}, u32[]{:S(2)}) copy-start(f32[1,8,128,128]{2,3,1,0:T(8,128)} %fusion.79) | copy-start | bytes 1572868
  300.3 5.9 %copy-start.25 = (f32[1,8,128,128]{2,3,1,0:T(8,128)S(1)}, f32[1,8,128,128]{2,3,1,0:T(8,128)}, u32[]{:S(2)}) copy-start(f32[1,8,128,128]{2,3,1,0:T(8,128)} %fusion.78) | copy-start | bytes 1572868
  305.4 17.8 %copy-start.19 = (bf16[128,2,8,128]{3,0,2,1:T(8,128)(2,1)S(1)}, bf16[128,2,8,128]{3,0,2,1:T(8,128)(2,1)}, u32[]{:S(2)}) copy-start(bf16[128,2,8,128]{3,0,2,1:T(8,128)(2,1)} %copy.46) | copy-start | bytes 1572868
  305.4 17.8 %copy-start.29 = (bf16[8,128,1601]{1,2,0:T(8,128)(2,1)S(1)}, bf16[8,128,1601]{1,2,0:T(8,128)(2,1)}, u32[]{:S(2)}) copy-start(bf16[8,128,1601]{1,2,0:T(8,128)(2,1)} %copy-done.28) | copy-start | bytes 9836548
  306.3 19.1 %copy-start.8 = (f32[2,8,128,128]{2,3,1,0:T(8,128)}, f32[2,8,128,128]{2,3,1,0:T(8,128)S(1)}, u32[]{:S(2)}) copy-start(f32[2,8,128,128]{2,3,1,0:T(8,128)S(1)} %pad_maximum_fusion.9) | copy-start | bytes 3145732
  306.3 18.0 %copy-start.31 = (bf16[8,128,1601]{1,2,0:T(8,128)(2,1)S(1)}, bf16[8,128,1601]{1,2,0:T(8,128)(2,1)}, u32[]{:S(2)}) copy-start(bf16[8,128,1601]{1,2,0:T(8,128)(2,1)} %copy-done.30) | copy-start | bytes 9836548
  306.4 19.0 %copy-start.10 = (f32[2,8,128,128]{2,3,1,0:T(8,128)}, f32[2,8,128,128]{2,3,1,0:T(8,128)S(1)}, u32[]{:S(2)}) copy-start(f32[2,8,128,128]{2,3,1,0:T(8,128)S(1)} %pad_maximum_fusion.8) | copy-start | bytes 3145732
  307.9 17.5 %copy-start.16 = (bf16[128,2,8,128]{3,0,2,1:T(8,128)(2,1)S(1)}, bf16[128,2,8,128]{3,0,2,1:T(8,128)(2,1)}, u32[]{:S(2)}) copy-start(bf16[128,2,8,128]{3,0,2,1:T(8,128)(2,1)} %copy.43) | copy-start | bytes 1572868
  307.9 53.6 %collective-permute-start.27 = (f32[2,128,2048]{1,2,0:T(8,128)}, f32[2,128,2048]{1,2,0:T(8,128)}, u32[]{:S(2)}, u32[]{:S(2)}) collective-permute-start(f32[2,128,2048]{1,2,0:T(8,128)} %pad_maximum_fusion.2), channel_id=1, source_target_pairs={{8,0},{12,4},{16,8},{20,12},{24,16},{28,20},{32,24},{36,28},{40,32... | collective-permute-start | bytes 6291464 | tf_op jit(solution)/shard_map/ppermute | solution.py:14
  309.4 72.4 %collective-permute-start.26 = (f32[2,128,2048]{1,2,0:T(8,128)}, f32[2,128,2048]{1,2,0:T(8,128)}, u32[]{:S(2)}, u32[]{:S(2)}) collective-permute-start(f32[2,128,2048]{1,2,0:T(8,128)} %pad_maximum_fusion.2), channel_id=1, source_target_pairs={{4,0},{8,4},{12,8},{16,12},{20,16},{24,20},{28,24},{32,28},{36,32}... | collective-permute-start | bytes 6291464 | tf_op jit(solution)/shard_map/ppermute | solution.py:14
  311.4 72.2 %collective-permute-start.25 = (f32[2,128,2048]{1,2,0:T(8,128)}, f32[2,128,2048]{1,2,0:T(8,128)}, u32[]{:S(2)}, u32[]{:S(2)}) collective-permute-start(f32[2,128,2048]{1,2,0:T(8,128)} %pad_maximum_fusion.2), channel_id=1, source_target_pairs={{0,4},{4,8},{8,12},{12,16},{16,20},{20,24},{24,28},{28,32},{32,36}... | collective-permute-start | bytes 6291464 | tf_op jit(solution)/shard_map/ppermute | solution.py:14
  316.8 68.5 %collective-permute-start.24 = (f32[2,128,2048]{1,2,0:T(8,128)}, f32[2,128,2048]{1,2,0:T(8,128)}, u32[]{:S(2)}, u32[]{:S(2)}) collective-permute-start(f32[2,128,2048]{1,2,0:T(8,128)} %pad_maximum_fusion.2), channel_id=1, source_target_pairs={{0,8},{4,12},{8,16},{12,20},{16,24},{20,28},{24,32},{28,36},{32,40... | collective-permute-start | bytes 6291464 | tf_op jit(solution)/shard_map/ppermute | solution.py:14
  324.3 3.3 slice-start.8
  325.4 2.2 slice-start.9
  325.4 2.2 copy-start.23
  326.5 2.5 slice-start.6
  330.9 6.0 %slice-start.4 = ((s8[6586368]{0:T(1024)(128)(4,1)}), s8[4194304]{0:T(1024)(128)(4,1)S(1)}, s32[]{:S(2)}) async-start(s8[6586368]{0:T(1024)(128)(4,1)} %bitcast.507), calls=%async_computation.4 | async-start | bytes 8388608
  332.3 4.6 slice-start.5
  333.7 4.6 slice-start
  339.9 5.4 %copy-start.3 = (bf16[2,1601,256]{1,2,0:T(8,128)(2,1)S(1)}, bf16[2,1601,256]{1,2,0:T(8,128)(2,1)}, u32[]{:S(2)}) copy-start(bf16[2,1601,256]{1,2,0:T(8,128)(2,1)} %copy-done.2) | copy-start | bytes 4918276
  363.1 23.8 %copy-start.7 = (f32[128,16,128]{0,2,1:T(8,128)S(1)}, f32[128,16,128]{0,2,1:T(8,128)}, u32[]{:S(2)}) copy-start(f32[128,16,128]{0,2,1:T(8,128)} %get-tuple-element.149) | copy-start | bytes 3145732
  363.1 23.8 %copy-start.9 = (f32[2,8,128,128]{2,3,1,0:T(8,128)S(1)}, f32[2,8,128,128]{2,3,1,0:T(8,128)}, u32[]{:S(2)}) copy-start(f32[2,8,128,128]{2,3,1,0:T(8,128)} %copy-done.8) | copy-start | bytes 3145732
  363.1 23.8 %copy-start.11 = (f32[2,8,128,128]{2,3,1,0:T(8,128)S(1)}, f32[2,8,128,128]{2,3,1,0:T(8,128)}, u32[]{:S(2)}) copy-start(f32[2,8,128,128]{2,3,1,0:T(8,128)} %copy-done.10) | copy-start | bytes 3145732
  363.2 23.8 %copy-start.26 = (f32[128]{0:T(128)S(1)}, f32[128]{0:T(128)}, u32[]{:S(2)}) copy-start(f32[128]{0:T(128)} %param.12) | copy-start | bytes 1540
  386.9 97.7 %copy-start.1 = (s32[64,128,5]{1,0,2:T(8,128)S(1)}, s32[64,128,5]{1,0,2:T(8,128)}, u32[]{:S(2)}) copy-start(s32[64,128,5]{1,0,2:T(8,128)} %param.18) | copy-start | bytes 491524
  (6 other events, 9.5 us)
where the time goes:
time: 491 us; the launch traced here: 486 us
  waiting for transfers between devices  139 us (28%)
  blocking collectives  94 us (19%)
  starting transfers between devices  83.6 us (17%)
  matrix products  58.2 us (12%)
  local copies, waits for them, and re-layouts  53.1 us (11%)
  other arithmetic  41.6 us (8%)
  between operations  16.3 us (3%)
    ppermute x28, waiting for transfers between devices, from_behind(): return lax.ppermute(value, axis, pairs)  139 us
    psum x1, blocking collectives, per_device(): lax.psum((query_gain_part, key_gain_part, gate_part), ('dp', 'heads'))  94 us
    ppermute x28, starting transfers between devices, from_behind(): return lax.ppermute(value, axis, pairs)  83.6 us
    unnamed x98, local copies, waits for them, and re-layouts  28 us
    dot_general x4, matrix products, head_backward(): jnp.einsum('hld,cd->hlc', grad_block, value_one, preferred_element_type=j...  20.7 us
    dot_general x4, matrix products, head_forward(): jnp.einsum('hld,cd->hlc', query_block, key_one, preferred_element_type=jn...  17.2 us
  transfers between devices with their start and end apart: 28, of which 10 were waited for; matrix products, arithmetic and copies ran while one was open for 14% of the time, Pallas kernels for 0%

commit v1 on v0

v1 whole, which is shorter than its diff:
```python
import functools

import jax
import jax.numpy as jnp
from jax import lax
from jax.experimental import pallas as pl
from jax.experimental.pallas import tpu as pltpu
from jax.sharding import PartitionSpec as P

EPSILON = 1e-05
NEGATIVE = -1e30
LOG2E = 1.4426950408889634
MESH = pl.DeviceIdType.MESH
F32 = jnp.float32
BF16 = jnp.bfloat16

GROUP = 4
DIM = 128
TEXT = 128
HEADS = 16
KV = 2
PER = HEADS // KV
CHUNKS = HEADS // 2
ROWS = 2 * TEXT
COLS = 1601
MAIN = 1600
PADDED = 1616
DEEP = 1664
SCALE = DIM ** (-0.5)


def blocks_of(size):
    out = [(a, min(size, MAIN - a)) for a in range(0, MAIN, size)]
    return out + [(MAIN, PADDED - MAIN)]


def dot(a, b):
    return jnp.dot(a, b, preferred_element_type=F32)


def fold(x, op):
    return op(x.reshape(x.shape[0] // 8, 8, x.shape[1]), axis=0)


def main_kernel(
    img_ref,
    gate_ref,
    qgain_ref,
    kgain_ref,
    tm_hbm,
    q_hbm,
    g_hbm,
    k_hbm,
    v_hbm,
    att_hbm,
    dq_hbm,
    dk_hbm,
    dv_hbm,
    part_ref,
    tm_ref,
    qbuf,
    gbuf,
    kraw,
    vraw,
    khat,
    vpad,
    turned,
    qh,
    qhT,
    gs,
    gsT,
    e_ref,
    p_ref,
    ds_ref,
    o_ref,
    dq_ref,
    dk_acc,
    dv_acc,
    m_ref,
    f_ref,
    d_ref,
    w_ref,
    stats,
    own_o,
    near_o,
    far_o,
    own_q,
    near_q,
    far_q,
    rnear_o,
    rfar_o,
    rnear_q,
    rfar_q,
    att_v,
    dq_v,
    load_sem,
    send_sem,
    recv_sem,
    stat_send,
    stat_recv,
    ret_send,
    ret_recv,
    out_sem,
):
    me = lax.axis_index("dp")
    group = me // GROUP
    j = me % GROUP
    base = group * GROUP
    inner = (j == 1) | (j == 2)
    outer = jnp.logical_not(inner)
    near = base + j + 1 - 2 * (j % 2)
    far = base + jnp.where(j < 2, 2, 1)
    far_slot = jnp.where(inner, 2, 3)
    side = jnp.where(j < 2, 0, 1)

    def slot_of(o):
        return o + side - 2 * o * side

    loads = [pltpu.make_async_copy(tm_hbm.at[pl.ds(base, GROUP)], tm_ref, load_sem.at[0])]
    loads.append(pltpu.make_async_copy(q_hbm.at[0], qbuf.at[0], load_sem.at[1]))
    loads.append(pltpu.make_async_copy(g_hbm.at[0], gbuf.at[0], load_sem.at[2]))
    for o in range(2):
        loads.append(pltpu.make_async_copy(k_hbm.at[slot_of(o)], kraw.at[o], load_sem.at[3 + o]))
        loads.append(pltpu.make_async_copy(v_hbm.at[slot_of(o)], vraw.at[o], load_sem.at[5 + o]))
    for c in loads:
        c.start()

    barrier = pltpu.get_barrier_semaphore()
    for step in range(1, GROUP):
        pl.semaphore_signal(
            barrier, inc=1, device_id={"dp": base + (j + step) % GROUP}, device_id_type=MESH
        )
    pl.semaphore_wait(barrier, GROUP - 1)

    def remote(src, dst, ss, rs, dev):
        return pltpu.make_async_remote_copy(
            src_ref=src, dst_ref=dst, send_sem=ss, recv_sem=rs,
            device_id={"dp": dev}, device_id_type=MESH,
        )

    sends = [
        remote(q_hbm.at[0], qbuf.at[1], send_sem.at[0], recv_sem.at[0, 1], near),
        remote(q_hbm.at[0], qbuf.at[far_slot], send_sem.at[1], recv_sem.at[0, far_slot], far),
        remote(g_hbm.at[0], gbuf.at[1], send_sem.at[2], recv_sem.at[1, 1], near),
        remote(g_hbm.at[0], gbuf.at[far_slot], send_sem.at[3], recv_sem.at[1, far_slot], far),
    ]
    for c in sends:
        c.start()

    def arrived(which, buf, slot):
        src = (q_hbm, g_hbm)[which]
        remote(src.at[0], buf.at[slot], send_sem.at[0], recv_sem.at[which, slot], near).wait_recv()

    docs, rels, ranks = [], [], []
    for o in range(2):
        local = 2 * j + slot_of(o)
        doc = img_ref[2 * base + local]
        rank = jnp.int32(0)
        for i in range(2 * GROUP):
            same = (img_ref[2 * base + i] == doc) & (i < local)
            rank = rank + jnp.where(same, 1, 0)
        doc = doc - base
        rel = jnp.where(
            doc == j, 0, jnp.where(doc == near - base, 1, jnp.where(doc == GROUP - 1 - j, 2, 3))
        )
        docs.append(doc)
        rels.append(rel)
        ranks.append(rank)
    gate = jnp.tanh(jnp.broadcast_to(gate_ref[...], (1, DIM)))

    @pl.when(outer)
    def _():
        for r in (2, 3):
            qbuf[r] = jnp.zeros((TEXT, HEADS * DIM), BF16)
            gbuf[r] = jnp.zeros((TEXT, HEADS * DIM), BF16)

    p_ref[PADDED:DEEP] = jnp.zeros((DEEP - PADDED, ROWS), BF16)
    ds_ref[PADDED:DEEP] = jnp.zeros((DEEP - PADDED, ROWS), BF16)

    loads[0].wait()
    seen = []
    lanes8 = lax.broadcasted_iota(jnp.int32, (TEXT, tm_ref.shape[2]), 1)
    for o in range(2):
        col = jnp.zeros((TEXT, 1), F32)
        for d in range(GROUP):
            hit = (lanes8 == ranks[o]) & (docs[o] == d)
            col = col + jnp.sum(jnp.where(hit, tm_ref[d], 0).astype(F32), axis=1, keepdims=True)
        seen.append(jnp.broadcast_to(col, (TEXT, TEXT)).T[0:1])

    tail_row = lax.broadcasted_iota(jnp.int32, (PADDED - MAIN, DIM), 0) == 0

    def unit_of(x):
        inverse = lax.rsqrt(jnp.mean(x * x, axis=1, keepdims=True) + EPSILON)
        return x * inverse, inverse

    def tail_of(ref, o, lanes):
        row = ref[o, MAIN:COLS, lanes].astype(F32)
        return jnp.where(tail_row, jnp.broadcast_to(row, (PADDED - MAIN, DIM)), 0.0)

    for o in range(2):
        loads[3 + 2 * o].wait()
        loads[4 + 2 * o].wait()

    def prep_kv(u, carry):
        o, k = u // KV, u % KV
        lanes = pl.ds(pl.multiple_of(k * DIM, DIM), DIM)
        for a, n in blocks_of(160):
            if a < MAIN:
                x = kraw[o, a : a + n, lanes].astype(F32)
                vpad[o, k, a : a + n, :] = vraw[o, a : a + n, lanes]
            else:
                x = tail_of(kraw, o, lanes)
                vpad[o, k, a : a + n, :] = tail_of(vraw, o, lanes).astype(BF16)
            unit, _ = unit_of(x)
            khat[o, k, a : a + n, :] = (unit * kgain_ref[...]).astype(BF16)
        return carry

    lax.fori_loop(0, 2 * KV, prep_kv, 0)

    def turn(src, o, k):
        for a in range(0, DEEP, DIM):
            if a + DIM <= PADDED:
                x = src[o, k, a : a + DIM, :].astype(F32)
            else:
                x = jnp.concatenate(
                    [src[o, k, a:PADDED, :].astype(F32), jnp.zeros((a + DIM - PADDED, DIM), F32)], axis=0
                )
            turned[:, a : a + DIM] = x.T.astype(BF16)

    def chosen(buf, o, count, lanes):
        x = buf[0, :, lanes].astype(F32)
        for r in range(1, count):
            x = jnp.where(rels[o] == r, buf[r, :, lanes].astype(F32), x)
        return x

    def prep_q(o, count):
        def body(hc, carry):
            x = chosen(qbuf, o, count, pl.ds(pl.multiple_of(hc * ROWS, ROWS), ROWS))
            for h in range(2):
                unit, _ = unit_of(x[:, h * DIM : (h + 1) * DIM])
                hat = unit * qgain_ref[...]
                qh[o, hc, h * TEXT : (h + 1) * TEXT, :] = hat.astype(BF16)
                qhT[o, hc, :, h * TEXT : (h + 1) * TEXT] = hat.T.astype(BF16)
            return carry

        lax.fori_loop(0, CHUNKS, body, 0)

    def prep_g(o, count):
        def body(hc, carry):
            x = chosen(gbuf, o, count, pl.ds(pl.multiple_of(hc * ROWS, ROWS), ROWS))
            for h in range(2):
                g = gate * x[:, h * DIM : (h + 1) * DIM]
                gs[o, hc, h * TEXT : (h + 1) * TEXT, :] = g.astype(BF16)
                gsT[o, hc, :, h * TEXT : (h + 1) * TEXT] = g.T.astype(BF16)
            return carry

        lax.fori_loop(0, CHUNKS, body, 0)

    def put_row(ref, o, hc, row):
        for h in range(2):
            ref[o, pl.ds(2 * hc + h, 1), :] = row[:, h * TEXT : (h + 1) * TEXT]

    def get_row(ref, o, hc):
        return jnp.concatenate([ref[o, pl.ds(2 * hc + h, 1), :] for h in range(2)], axis=1)

    tail_mask = lax.broadcasted_iota(jnp.int32, (PADDED - MAIN, ROWS), 0) == 0

    def forward(o):
        def per_kv(k, carry):
            turn(vpad, o, k)

            def chunk(c, carry):
                hc = k * (PER // 2) + c
                i = o * CHUNKS + hc
                qT = qhT[o, hc]
                top = jnp.full((8, ROWS), -jnp.inf, F32)
                for a, n in blocks_of(400):
                    s = dot(khat[o, k, a : a + n, :], qT)
                    if a == MAIN:
                        s = jnp.where(tail_mask, s, -jnp.inf)
                    e_ref[i, a : a + n, :] = s
                    top = jnp.maximum(top, fold(s, jnp.max))
                top = jnp.max(top, axis=0, keepdims=True)
                total = jnp.zeros((8, ROWS), F32)
                for a, n in blocks_of(80):
                    e = jnp.exp2((e_ref[i, a : a + n, :] - top) * (SCALE * LOG2E))
                    e_ref[i, a : a + n, :] = e
                    total = total + fold(e, jnp.sum)
                total = jnp.sum(total, axis=0, keepdims=True)
                inverse = 1.0 / total
                for a, n in blocks_of(80):
                    p_ref[a : a + n, :] = (e_ref[i, a : a + n, :] * inverse).astype(BF16)
                o_ref[o, hc] = dot(turned[...], p_ref[...])
                put_row(m_ref, o, hc, top * SCALE)
                put_row(w_ref, o, hc, top * SCALE + jnp.log(total))
                return carry

            lax.fori_loop(0, PER // 2, chunk, 0)
            return carry

        lax.fori_loop(0, KV, per_kv, 0)

    loads[1].wait()
    arrived(0, qbuf, 1)

    @pl.when(inner)
    def _():
        arrived(0, qbuf, 2)

    prep_q(0, 3)
    forward(0)

    @pl.when(inner)
    def _():
        arrived(0, qbuf, 3)

    prep_q(1, 4)
    forward(1)

    loads[2].wait()
    arrived(1, gbuf, 1)

    @pl.when(inner)
    def _():
        arrived(1, gbuf, 2)
        arrived(1, gbuf, 3)

    for o in range(2):
        prep_g(o, 3 + o)

        def delta(hc, carry):
            prod = o_ref[o, hc] * gsT[o, hc].astype(F32)
            put_row(d_ref, o, hc, jnp.sum(prod, axis=0, keepdims=True))
            return carry

        lax.fori_loop(0, CHUNKS, delta, 0)
        saw = jnp.broadcast_to(seen[o], (HEADS, TEXT)) > 0.0
        stats[j, slot_of(o), 0] = jnp.where(saw, w_ref[o], NEGATIVE)
        stats[j, slot_of(o), 1] = jnp.where(saw, d_ref[o], 0.0)

    swaps = []
    for step in range(1, GROUP):
        swaps.append(
            remote(
                stats.at[j], stats.at[j], stat_send.at[step - 1], stat_recv.at[j],
                base + (j + step) % GROUP,
            )
        )
    for c in swaps:
        c.start()
    for step in range(1, GROUP):
        other = (j + step) % GROUP
        remote(stats.at[j], stats.at[other], stat_send.at[0], stat_recv.at[other], near).wait_recv()

    for o in range(2):
        mine = [img_ref[2 * base + i] - base == docs[o] for i in range(2 * GROUP)]
        lses = [
            jnp.where(mine[i], stats[i // 2, i % 2, 0], 2.0 * NEGATIVE) for i in range(2 * GROUP)
        ]
        top = functools.reduce(jnp.maximum, lses)
        terms = [jnp.exp(x - top) for x in lses]
        total = functools.reduce(jnp.add, terms)
        weighted = [
            t * jnp.where(mine[i], stats[i // 2, i % 2, 1], 0.0) for i, t in enumerate(terms)
        ]
        saw = jnp.broadcast_to(seen[o], (HEADS, TEXT)) > 0.0
        own = jnp.where(saw, w_ref[o], NEGATIVE)
        d_ref[o] = functools.reduce(jnp.add, weighted) / total
        f_ref[o] = jnp.where(saw, jnp.exp(m_ref[o] - (top + jnp.log(total))), 0.0)
        w_ref[o] = jnp.where(saw, jnp.exp(own - top) / total, 0.0)

    def share(pair, own_b, near_b, far_b, k, lanes):
        def total(r):
            a = jnp.where(rels[0] == r, pair[0], 0.0)
            return a + jnp.where(rels[1] == r, pair[1], 0.0)

        own_b[k, :, lanes] = total(0)
        near_b[k, :, lanes] = total(1)
        far_b[0, k, :, lanes] = total(2).astype(BF16)
        far_b[1, k, :, lanes] = total(3).astype(BF16)

    def returns(which, k, near_b, far_b, rnear_b, rfar_b):
        one = remote(
            near_b.at[k], rnear_b.at[k], ret_send.at[which, k, 0], ret_recv.at[which, k, 0], near
        )
        two = [
            remote(
                far_b.at[r, k], rfar_b.at[k], ret_send.at[which, k, 1 + r],
                ret_recv.at[which, k, 1], base + jnp.where(j == 1, 2 + r, 1 - r),
            )
            for r in range(2)
        ]
        return one, two

    def start_returns(*args):
        one, two = returns(*args)
        one.start()

        @pl.when(inner)
        def _():
            for c in two:
                c.start()

    def finish_sends(*args):
        one, two = returns(*args)
        one.wait_send()

        @pl.when(inner)
        def _():
            for c in two:
                c.wait_send()

    def wait_returns(*args):
        one, two = returns(*args)
        one.wait_recv()
        two[0].wait_recv()

    o_args = (near_o, far_o, rnear_o, rfar_o)
    q_args = (near_q, far_q, rnear_q, rfar_q)

    def give_out(k, carry):
        def body(c, carry):
            hc = k * (PER // 2) + c
            pair = []
            for o in range(2):
                x = o_ref[o, hc] * get_row(w_ref, o, hc)
                pair.append(jnp.concatenate([x[:, :TEXT].T, x[:, TEXT:].T], axis=1))
            share(pair, own_o, near_o, far_o, k, pl.ds(pl.multiple_of(c * ROWS, ROWS), ROWS))
            return carry

        lax.fori_loop(0, PER // 2, body, 0)
        start_returns(0, k, *o_args)
        return carry

    lax.fori_loop(0, KV, give_out, 0)

    def backward(k, kgain_sum):
        lanes = pl.ds(pl.multiple_of(k * DIM, DIM), DIM)

        def per_slot(o, kgain_sum):
            turn(khat, o, k)
            dk_acc[...] = jnp.zeros_like(dk_acc)
            dv_acc[...] = jnp.zeros_like(dv_acc)

            def chunk(c, carry):
                hc = k * (PER // 2) + c
                i = o * CHUNKS + hc
                gT = gsT[o, hc]
                grows = gs[o, hc]
                qrows = qh[o, hc]
                factor = get_row(f_ref, o, hc)
                delta = get_row(d_ref, o, hc)
                for a, n in blocks_of(160):
                    dp = dot(vpad[o, k, a : a + n, :], gT)
                    p = e_ref[i, a : a + n, :] * factor
                    pb = p.astype(BF16)
                    ds = (p * (dp - delta)).astype(BF16)
                    ds_ref[a : a + n, :] = ds
                    dv_acc[a : a + n, :] += dot(pb, grows)
                    dk_acc[a : a + n, :] += dot(ds, qrows)
                x = dot(turned[...], ds_ref[...])
                dq_ref[o, c] = jnp.concatenate([x[:, :TEXT].T, x[:, TEXT:].T], axis=1)
                return carry

            lax.fori_loop(0, PER // 2, chunk, 0)

            for a, n in blocks_of(160):
                last = a == MAIN
                x = tail_of(kraw, o, lanes) if last else kraw[o, a : a + n, lanes].astype(F32)
                up = dk_acc[a : a + n, :] * SCALE
                unit, inverse = unit_of(x)
                scaled = up * kgain_ref[...]
                back = inverse * (scaled - unit * jnp.mean(scaled * unit, axis=1, keepdims=True))
                kgain_sum = kgain_sum + fold(up * unit, jnp.sum)
                value = dv_acc[a : a + n, :]
                if last:
                    back, value, n = back[:1], value[:1], 1
                kraw[o, a : a + n, lanes] = back.astype(BF16)
                vraw[o, a : a + n, lanes] = value.astype(BF16)
            return kgain_sum

        kgain_sum = lax.fori_loop(0, 2, per_slot, kgain_sum)

        def body(c, carry):
            share(
                [dq_ref[0, c], dq_ref[1, c]], own_q, near_q, far_q, k,
                pl.ds(pl.multiple_of(c * ROWS, ROWS), ROWS),
            )
            return carry

        lax.fori_loop(0, PER // 2, body, 0)
        start_returns(1, k, *q_args)
        return kgain_sum

    kgain_sum = lax.fori_loop(0, KV, backward, jnp.zeros((8, DIM), F32))

    outs = []
    for o in range(2):
        outs.append(pltpu.make_async_copy(kraw.at[o], dk_hbm.at[slot_of(o)], out_sem.at[2 * o]))
        outs.append(pltpu.make_async_copy(vraw.at[o], dv_hbm.at[slot_of(o)], out_sem.at[2 * o + 1]))
    for c in outs:
        c.start()

    for k in range(KV):
        wait_returns(0, k, *o_args)

    def attend(k, gate_sum):
        for c in range(PER):
            lanes = slice(c * DIM, (c + 1) * DIM)
            full = pl.ds(pl.multiple_of(k * PER * DIM + c * DIM, DIM), DIM)
            merged = own_o[k, :, lanes] + rnear_o[k, :, lanes] + rfar_o[k, :, lanes].astype(F32)
            att_v[:, full] = (gate * merged).astype(BF16)
            gate_sum = gate_sum + fold(gbuf[0, :, full].astype(F32) * merged, jnp.sum)
        return gate_sum

    gate_sum = lax.fori_loop(0, KV, attend, jnp.zeros((8, DIM), F32))
    out_att = pltpu.make_async_copy(att_v, att_hbm.at[0], out_sem.at[4])
    out_att.start()

    for k in range(KV):
        wait_returns(1, k, *q_args)

    def finish(k, qgain_sum):
        for c in range(PER):
            lanes = slice(c * DIM, (c + 1) * DIM)
            full = pl.ds(pl.multiple_of(k * PER * DIM + c * DIM, DIM), DIM)
            hat = own_q[k, :, lanes] + rnear_q[k, :, lanes] + rfar_q[k, :, lanes].astype(F32)
            hat = hat * SCALE
            unit, inverse = unit_of(qbuf[0, :, full].astype(F32))
            scaled = hat * qgain_ref[...]
            back = inverse * (scaled - unit * jnp.mean(scaled * unit, axis=1, keepdims=True))
            dq_v[:, full] = back.astype(BF16)
            qgain_sum = qgain_sum + fold(hat * unit, jnp.sum)
        return qgain_sum

    qgain_sum = lax.fori_loop(0, KV, finish, jnp.zeros((8, DIM), F32))
    out_dq = pltpu.make_async_copy(dq_v, dq_hbm.at[0], out_sem.at[5])
    out_dq.start()

    row = lax.broadcasted_iota(jnp.int32, (8, DIM), 0)
    gate_total = jnp.sum(jnp.sum(gate_sum, axis=0, keepdims=True), axis=1, keepdims=True)
    part_ref[...] = jnp.where(
        row == 0,
        jnp.sum(qgain_sum, axis=0, keepdims=True),
        jnp.where(
            row == 1,
            jnp.sum(kgain_sum, axis=0, keepdims=True),
            (1.0 - gate * gate) * gate_total,
        ),
    )

    for c in sends:
        c.wait_send()
    for c in swaps:
        c.wait_send()
    for k in range(KV):
        finish_sends(0, k, *o_args)
        finish_sends(1, k, *q_args)
    for c in outs:
        c.wait()
    out_att.wait()
    out_dq.wait()


def run_main(img, gate, qgain, kgain, text_mask, q, g, kk, vv):
    vm = pltpu.VMEM
    dma = pltpu.SemaphoreType.DMA
    half = (KV, TEXT, PER * DIM)
    slots = text_mask.shape[2]
    scratch = [
        vm((GROUP, TEXT, slots), jnp.int32),
        vm((4, TEXT, HEADS * DIM), BF16),
        vm((4, TEXT, HEADS * DIM), BF16),
        vm((2, COLS, KV * DIM), BF16),
        vm((2, COLS, KV * DIM), BF16),
        vm((2, KV, PADDED, DIM), BF16),
        vm((2, KV, PADDED, DIM), BF16),
        vm((DIM, DEEP), BF16),
        vm((2, CHUNKS, ROWS, DIM), BF16),
        vm((2, CHUNKS, DIM, ROWS), BF16),
        vm((2, CHUNKS, ROWS, DIM), BF16),
        vm((2, CHUNKS, DIM, ROWS), BF16),
        vm((2 * CHUNKS, PADDED, ROWS), F32),
        vm((DEEP, ROWS), BF16),
        vm((DEEP, ROWS), BF16),
        vm((2, CHUNKS, DIM, ROWS), F32),
        vm((2, PER // 2, TEXT, ROWS), F32),
        vm((PADDED, DIM), F32),
        vm((PADDED, DIM), F32),
        vm((2, HEADS, TEXT), F32),
        vm((2, HEADS, TEXT), F32),
        vm((2, HEADS, TEXT), F32),
        vm((2, HEADS, TEXT), F32),
        vm((GROUP, 2, 2, HEADS, TEXT), F32),
        vm(half, F32),
        vm(half, F32),
        vm((2,) + half, BF16),
        vm(half, F32),
        vm(half, F32),
        vm((2,) + half, BF16),
        vm(half, F32),
        vm(half, BF16),
        vm(half, F32),
        vm(half, BF16),
        vm((TEXT, HEADS * DIM), BF16),
        vm((TEXT, HEADS * DIM), BF16),
        dma((7,)),
        dma((4,)),
        dma((2, 4)),
        dma((3,)),
        dma((4,)),
        dma((2, KV, 3)),
        dma((2, KV, 2)),
        dma((6,)),
    ]
    hbm = pl.BlockSpec(memory_space=pl.ANY)
    vmem = pl.BlockSpec(memory_space=pltpu.VMEM)
    return pl.pallas_call(
        main_kernel,
        out_shape=(
            jax.ShapeDtypeStruct(q.shape, BF16),
            jax.ShapeDtypeStruct(q.shape, BF16),
            jax.ShapeDtypeStruct(kk.shape, BF16),
            jax.ShapeDtypeStruct(vv.shape, BF16),
            jax.ShapeDtypeStruct((8, DIM), F32),
        ),
        in_specs=[pl.BlockSpec(memory_space=pltpu.SMEM), vmem, vmem, vmem] + [hbm] * 5,
        out_specs=(hbm, hbm, hbm, hbm, vmem),
        scratch_shapes=scratch,
        compiler_params=pltpu.CompilerParams(
            collective_id=0, has_side_effects=True, vmem_limit_bytes=64 * 1024 * 1024
        ),
    )(img, gate, qgain, kgain, text_mask, q, g, kk, vv)


def stages_of(sizes):
    low = min(8, sizes["dp"])
    out = [("dp", 1, low)]
    if sizes["heads"] > 1:
        out.append(("heads", 1, sizes["heads"]))
    if sizes["dp"] > low:
        out.append(("dp", low, sizes["dp"] // low))
    return out


def sum_kernel(stages, part_ref, qg_out, kg_out, gate_out, *scratch):
    bufs, (send_sem, recv_sem) = scratch[: len(stages)], scratch[len(stages) :]

    def place(stage):
        axis, stride, count = stage
        me = lax.axis_index(axis)
        mine = (me // stride) % count
        return axis, stride, count, me, mine, me - mine * stride

    barrier = pltpu.get_barrier_semaphore()
    partners = 0
    for stage in stages:
        axis, stride, count, me, mine, low = place(stage)
        for step in range(1, count):
            other = low + stride * ((mine + step) % count)
            pl.semaphore_signal(barrier, inc=1, device_id={axis: other}, device_id_type=MESH)
            partners += 1
    pl.semaphore_wait(barrier, partners)

    value = part_ref[...]
    for n, stage in enumerate(stages):
        axis, stride, count, me, mine, low = place(stage)
        buf = bufs[n]
        buf[mine] = value
        copies = []
        for step in range(1, count):
            other = low + stride * ((mine + step) % count)
            c = pltpu.make_async_remote_copy(
                src_ref=buf.at[mine], dst_ref=buf.at[mine], send_sem=send_sem.at[n, step],
                recv_sem=recv_sem.at[n, mine], device_id={axis: other}, device_id_type=MESH,
            )
            c.start()
            copies.append(c)
        for step in range(1, count):
            src = (mine + step) % count
            pltpu.make_async_remote_copy(
                src_ref=buf.at[src], dst_ref=buf.at[src], send_sem=send_sem.at[n, step],
                recv_sem=recv_sem.at[n, src], device_id={axis: low + stride * src},
                device_id_type=MESH,
            ).wait_recv()
        value = buf[0]
        for i in range(1, count):
            value = value + buf[i]
        for c in copies:
            c.wait_send()
    qg_out[...] = value[0:1]
    kg_out[...] = value[1:2]
    gate_out[...] = value[2:3, 0:1]


def run_sum(part, sizes):
    stages = stages_of(sizes)
    vmem = pl.BlockSpec(memory_space=pltpu.VMEM)
    most = max(s[2] for s in stages)
    return pl.pallas_call(
        functools.partial(sum_kernel, stages),
        out_shape=(
            jax.ShapeDtypeStruct((1, DIM), F32),
            jax.ShapeDtypeStruct((1, DIM), F32),
            jax.ShapeDtypeStruct((1, 1), F32),
        ),
        in_specs=[vmem],
        out_specs=(vmem, vmem, vmem),
        scratch_shapes=[pltpu.VMEM((s[2], 8, DIM), F32) for s in stages]
        + [pltpu.SemaphoreType.DMA((len(stages), most))] * 2,
        compiler_params=pltpu.CompilerParams(collective_id=1, has_side_effects=True),
    )(part)


def solution(mesh):
    sizes = dict(mesh.shape)

    def per_device(q, qgain, kk, vv, kgain, gate, img, text_mask, g):
        att, dq, dk, dv, part = run_main(
            img, gate.reshape(1, 1), qgain.reshape(1, DIM), kgain.reshape(1, DIM), text_mask,
            q, g, kk, vv,
        )
        qg, kg, gt = run_sum(part, sizes)
        return att, dq, dk, dv, qg.reshape(DIM), kg.reshape(DIM), gt.reshape(1)

    split = P("dp", None, "heads")
    return jax.shard_map(
        per_device,
        mesh=mesh,
        in_specs=(split, P(), split, split, P(), P(), P(), P(), split),
        out_specs=(split, split, split, split, P(), P(), P()),
        check_vma=False,
    )
```

time: 491 us -> 144 us (0.29); the launches traced: 486 us -> 144 us
  waiting for transfers between devices: 139 us -> 0 us
  Pallas kernels: 0 us -> 108 us
  blocking collectives: 94 us -> 0 us
  starting transfers between devices: 83.6 us -> 0 us
  matrix products: 58.2 us -> 0 us
  other arithmetic: 41.6 us -> 0 us
  local copies, waits for them, and re-layouts: 53.1 us -> 32.9 us
  between operations: 16.3 us -> 3.21 us
    ppermute x28 -> x0, waiting for transfers between devices: 139 us -> none  [from_behind(): return lax.ppermute(value, axis, pairs)]
    pallas_call x0 -> x2, Pallas kernels: none -> 108 us  [the longest x1 85.8 us: run_main(): pl.pallas_call(main_kernel, out_shape=(jax.ShapeDtypeStruct(q.shape, BF16...]
    psum x1 -> x0, blocking collectives: 94 us -> none  [per_device(): lax.psum((query_gain_part, key_gain_part, gate_part), ('dp', 'heads'))]
    ppermute x28 -> x0, starting transfers between devices: 83.6 us -> none  [from_behind(): return lax.ppermute(value, axis, pairs)]
    dot_general x24 -> x0, matrix products: 58.2 us -> none  [the longest x4 20.7 us: head_backward(): jnp.einsum('hld,cd->hlc', grad_block, value_one, preferred_element_type=j...]
    reduce_sum x16 -> x0, other arithmetic: 18.2 us -> none  [the longest x3 5.47 us: unit_back(): jnp.sum((upstream * normed).reshape(-1, normed.shape[-1]), axis=0)]
    select_n x14 -> x0, other arithmetic: 12.3 us -> none  [the longest x4 6.72 us: per_device(): jnp.where(source_usable(offset, slot_number), query_from_back[offset][slo...]
    another operation x6 -> x0, local copies, waits for them, and re-layouts: 9.29 us -> none  [the longest x2 4.44 us: per_device(): key_slots.append(jnp.stack(key_list, axis=1))]
  transfers between devices with their start and end apart: 28 -> 0, of which waited for: 10 -> 0; matrix products, arithmetic and copies ran while one was open for 14% -> 0% of each run, Pallas kernels for 0% -> 0%
where the time goes in v1:
time: 144 us
  Pallas kernels  108 us (75%)
  local copies, waits for them, and re-layouts  32.9 us (23%)
  between operations  3.21 us (2%)
    pallas_call x1, Pallas kernels, run_main(): pl.pallas_call(main_kernel, out_shape=(jax.ShapeDtypeStruct(q.shape, BF16...  85.8 us
    unnamed x23, local copies, waits for them, and re-layouts  32.9 us
    pallas_call x1, Pallas kernels, run_sum(): pl.pallas_call(functools.partial(sum_kernel, stages), out_shape=(jax.Shap...  22.1 us

profile of v1, /device:TPU:1, one launch (start us, length us, event | category | flops | bytes accessed | tf_op | source)
XLA Modules:
  0.0 143.9 jit_solution(12461576196663466622)
XLA Ops:
  0.6 0.0 copy-start.1
  1.4 2.9 %copy.17.k_hbm = bf16[2,1601,256]{2,1,0:T(8,128)(2,1)} copy(bf16[2,1601,256]{2,0,1:T(2,128)(2,1)} %param.11) | data formatting | bytes 3278848 | tf_op args[2]
  4.3 0.0 copy-done.1
  4.3 0.0 copy-start.4
  4.3 1.4 copy.18.v_hbm
  5.7 0.0 copy-done.4
  5.7 2.7 %copy.16.tm_hbm = s32[64,128,5]{2,1,0:T(8,128)} copy(s32[64,128,5]{1,0,2:T(8,128)S(1)} %copy-done.4) | data formatting | bytes 327680 | tf_op args[7]
  8.4 85.8 %shard_map.144 = (bf16[1,128,2048]{2,1,0:T(8,128)(2,1)}, bf16[1,128,2048]{2,1,0:T(8,128)(2,1)}, bf16[2,1601,256]{2,1,0:T(8,128)(2,1)}, bf16[2,1601,256]{2,1,0:T(8,128)(2,1)}, f32[8,128]{1,0:T(8,128)}) custom-call(s32[128]{0:T(128)} %img_ref.1, f32[1,1]{1,0:T(1,128)} %bitcast.6.gate_ref, f32[1,128]{1,0:T(1,128)} %bitcast.7, f32[1,128]{1,0:T(1,128)} %bitcast.8, ...), custom_call_target="tpu_custom_call" | custom-call | tf_op jit(solution)/shard_map/pallas_call | solution.py:618
  94.2 22.1 %shard_map.145 = (f32[1,128]{1,0:T(1,128)}, f32[1,128]{1,0:T(1,128)}, f32[1,1]{1,0:T(1,128)}) custom-call(f32[8,128]{1,0:T(8,128)} %get-tuple-element.19.part_ref), custom_call_target="tpu_custom_call" | custom-call | tf_op jit(solution)/shard_map/pallas_call | solution.py:700
  116.3 0.0 copy-start
  116.3 13.4 %copy.19 = bf16[2,1601,256]{2,0,1:T(2,128)(2,1)} copy(bf16[2,1601,256]{2,1,0:T(8,128)(2,1)} %get-tuple-element.25) | data formatting | bytes 3278848
  129.6 0.0 copy-done
  129.6 0.0 copy-start.3
  129.7 0.0 copy-start.2
  129.7 9.9 %copy.20 = bf16[2,1601,256]{2,0,1:T(2,128)(2,1)} copy(bf16[2,1601,256]{2,1,0:T(8,128)(2,1)S(1)} %copy-done) | data formatting | bytes 3278848
  139.5 0.0 copy-done.3
  139.5 0.0 copy-start.6
  139.5 0.0 copy-start.5
  139.5 0.8 copy.27
  140.3 0.0 copy-done.2
  140.3 0.8 copy.28
  141.1 0.0 copy-done.6
  141.1 0.5 copy.29
  141.7 0.0 copy-done.5
  141.7 0.5 copy.30
Async XLA Ops:
  0.6 3.7 %copy-start.1 = (bf16[2,1601,256]{2,0,1:T(2,128)(2,1)S(1)}, bf16[2,1601,256]{2,0,1:T(2,128)(2,1)}, u32[]{:S(2)}) copy-start(bf16[2,1601,256]{2,0,1:T(2,128)(2,1)} %param.12) | copy-start | bytes 4918276
  4.3 1.4 copy-start.4
  116.3 13.4 %copy-start = (bf16[2,1601,256]{2,1,0:T(8,128)(2,1)S(1)}, bf16[2,1601,256]{2,1,0:T(8,128)(2,1)}, u32[]{:S(2)}) copy-start(bf16[2,1601,256]{2,1,0:T(8,128)(2,1)} %get-tuple-element.26) | copy-start | bytes 4918276
  129.6 9.9 %copy-start.3 = (bf16[1,128,2048]{2,1,0:T(8,128)(2,1)S(1)}, bf16[1,128,2048]{2,1,0:T(8,128)(2,1)}, u32[]{:S(2)}) copy-start(bf16[1,128,2048]{2,1,0:T(8,128)(2,1)} %get-tuple-element.37) | copy-start | bytes 1572868
  129.7 10.7 %copy-start.2 = (bf16[1,128,2048]{2,1,0:T(8,128)(2,1)S(1)}, bf16[1,128,2048]{2,1,0:T(8,128)(2,1)}, u32[]{:S(2)}) copy-start(bf16[1,128,2048]{2,1,0:T(8,128)(2,1)} %get-tuple-element.38) | copy-start | bytes 1572868
  139.5 1.6 %copy-start.6 = (f32[1,128]{1,0:T(1,128)S(1)}, f32[1,128]{1,0:T(1,128)}, u32[]{:S(2)}) copy-start(f32[1,128]{1,0:T(1,128)} %get-tuple-element.20) | copy-start | bytes 1540
  139.5 2.1 %copy-start.5 = (f32[1,128]{1,0:T(1,128)S(1)}, f32[1,128]{1,0:T(1,128)}, u32[]{:S(2)}) copy-start(f32[1,128]{1,0:T(1,128)} %get-tuple-element.21) | copy-start | bytes 1540

commit v2 on v1

v2 whole, which is shorter than its diff:
```python
import functools

import jax
import jax.numpy as jnp
from jax import lax
from jax.experimental import pallas as pl
from jax.experimental.pallas import tpu as pltpu
from jax.sharding import PartitionSpec as P

EPSILON = 1e-05
NEGATIVE = -1e30
LOG2E = 1.4426950408889634
MESH = pl.DeviceIdType.MESH
F32 = jnp.float32
BF16 = jnp.bfloat16

GROUP = 4
DIM = 128
TEXT = 128
HEADS = 16
KV = 2
PER = HEADS // KV
CHUNKS = HEADS // 2
ROWS = 2 * TEXT
SPAN = PER * TEXT
COLS = 1601
MAIN = 1600
PADDED = 1616
DEEP = 1664
SCALE = DIM ** (-0.5)


def dot(a, b):
    return jnp.dot(a, b, preferred_element_type=F32)


def fold(x, op):
    return op(x.reshape(x.shape[0] // 8, 8, x.shape[1]), axis=0)


def place(stage):
    axis, stride, count = stage
    me = lax.axis_index(axis)
    mine = (me // stride) % count
    return axis, stride, count, mine, me - mine * stride


def main_kernel(
    stages,
    img_ref,
    gate_ref,
    qgain_ref,
    kgain_ref,
    tm_hbm,
    q_hbm,
    g_hbm,
    k_hbm,
    v_hbm,
    att_hbm,
    dq_hbm,
    dk_hbm,
    dv_hbm,
    qg_out,
    kg_out,
    gate_out,
    tm_ref,
    qbuf,
    gbuf,
    kraw,
    vraw,
    wide_k,
    wide_v,
    khat,
    vpad,
    turned_k,
    turned_v,
    qh,
    qhT,
    gs,
    gsT,
    e_ref,
    o_ref,
    dq_ref,
    x_acc,
    m_ref,
    f_ref,
    d_ref,
    w_ref,
    gam_ref,
    stats,
    own_o,
    near_o,
    far_o,
    own_q,
    near_q,
    far_q,
    rnear_o,
    rfar_o,
    rnear_q,
    rfar_q,
    att_v,
    dq_v,
    load_sem,
    send_sem,
    recv_sem,
    stat_send,
    stat_recv,
    ret_send,
    ret_recv,
    out_sem,
    sum_send,
    sum_recv,
    *sum_bufs,
):
    me = lax.axis_index("dp")
    group = me // GROUP
    j = me % GROUP
    base = group * GROUP
    base8 = pl.multiple_of(me // 8 * 8, 8)
    inner = (j == 1) | (j == 2)
    outer = jnp.logical_not(inner)
    near = base + j + 1 - 2 * (j % 2)
    far = base + jnp.where(j < 2, 2, 1)
    far_slot = jnp.where(inner, 2, 3)
    side = jnp.where(j < 2, 0, 1)

    def slot_of(o):
        return o + side - 2 * o * side

    loads = [pltpu.make_async_copy(tm_hbm.at[:, pl.ds(base8, 8), :], tm_ref, load_sem.at[0])]
    loads.append(pltpu.make_async_copy(q_hbm.at[0], qbuf.at[0], load_sem.at[1]))
    loads.append(pltpu.make_async_copy(g_hbm.at[0], gbuf.at[0], load_sem.at[2]))
    loads.append(pltpu.make_async_copy(k_hbm, kraw, load_sem.at[3]))
    loads.append(pltpu.make_async_copy(v_hbm, vraw, load_sem.at[4]))
    for c in loads:
        c.start()

    barrier = pltpu.get_barrier_semaphore()
    for step in range(1, GROUP):
        pl.semaphore_signal(
            barrier, inc=1, device_id={"dp": base + (j + step) % GROUP}, device_id_type=MESH
        )
    partners = GROUP - 1
    for stage in stages:
        axis, stride, count, mine, low = place(stage)
        for step in range(1, count):
            other = low + stride * ((mine + step) % count)
            pl.semaphore_signal(barrier, inc=1, device_id={axis: other}, device_id_type=MESH)
            partners += 1
    pl.semaphore_wait(barrier, partners)

    def remote(src, dst, ss, rs, dev):
        return pltpu.make_async_remote_copy(
            src_ref=src, dst_ref=dst, send_sem=ss, recv_sem=rs,
            device_id={"dp": dev}, device_id_type=MESH,
        )

    sends = [
        remote(q_hbm.at[0], qbuf.at[1], send_sem.at[0], recv_sem.at[0, 1], near),
        remote(q_hbm.at[0], qbuf.at[far_slot], send_sem.at[1], recv_sem.at[0, far_slot], far),
        remote(g_hbm.at[0], gbuf.at[1], send_sem.at[2], recv_sem.at[1, 1], near),
        remote(g_hbm.at[0], gbuf.at[far_slot], send_sem.at[3], recv_sem.at[1, far_slot], far),
    ]
    sends[0].start()

    @pl.when(inner)
    def _():
        sends[1].start()

    def arrived(which, buf, slot):
        src = (q_hbm, g_hbm)[which]
        remote(src.at[0], buf.at[slot], send_sem.at[0], recv_sem.at[which, slot], near).wait_recv()

    docs, rels, ranks = [], [], []
    for o in range(2):
        local = 2 * j + slot_of(o)
        doc = img_ref[2 * base + local]
        rank = jnp.int32(0)
        for i in range(2 * GROUP):
            same = (img_ref[2 * base + i] == doc) & (i < local)
            rank = rank + jnp.where(same, 1, 0)
        doc = doc - base
        rel = jnp.where(
            doc == j, 0, jnp.where(doc == near - base, 1, jnp.where(doc == GROUP - 1 - j, 2, 3))
        )
        docs.append(doc)
        rels.append(rel)
        ranks.append(rank)
    gate = jnp.tanh(jnp.broadcast_to(gate_ref[...], (1, DIM)))

    @pl.when(outer)
    def _():
        for r in (2, 3):
            qbuf[r] = jnp.zeros((TEXT, HEADS * DIM), BF16)
            gbuf[r] = jnp.zeros((TEXT, HEADS * DIM), BF16)


    loads[0].wait()
    seen = []
    rank_at = lax.broadcasted_iota(jnp.int32, tm_ref.shape, 0)
    doc_at = lax.broadcasted_iota(jnp.int32, tm_ref.shape, 1)
    for o in range(2):
        hit = (rank_at == ranks[o]) & (doc_at == docs[o] + (base - base8))
        row = jnp.sum(jnp.where(hit, tm_ref[...], 0).astype(F32), axis=0)
        seen.append(jnp.sum(row, axis=0, keepdims=True))

    tail_row = lax.broadcasted_iota(jnp.int32, (PADDED - MAIN, DIM), 0) == 0

    def unit_of(x):
        inverse = lax.rsqrt(jnp.mean(x * x, axis=1, keepdims=True) + EPSILON)
        return x * inverse, inverse

    def rows_of(o, k, a, n):
        return pl.ds(4 * a + 2 * k + slot_of(o), n, stride=4)

    def tail_of(ref, o, k):
        row = ref[pl.ds(4 * MAIN + 2 * k + slot_of(o), 1), :]
        return jnp.where(tail_row, jnp.broadcast_to(row, (PADDED - MAIN, DIM)), 0.0)

    def widen(raw, wide):
        rows = raw.reshape(4 * COLS, DIM)

        def body(i, carry):
            at = pl.ds(pl.multiple_of(i * 320, 320), 320)
            wide[at, :] = rows[at, :].astype(F32)
            return carry

        lax.fori_loop(0, 4 * MAIN // 320, body, 0)
        wide[4 * MAIN : 4 * COLS, :] = rows[4 * MAIN : 4 * COLS, :].astype(F32)

    def narrow(wide, raw):
        rows = raw.reshape(4 * COLS, DIM)

        def body(i, carry):
            at = pl.ds(pl.multiple_of(i * 320, 320), 320)
            rows[at, :] = wide[at, :].astype(BF16)
            return carry

        lax.fori_loop(0, 4 * MAIN // 320, body, 0)
        rows[4 * MAIN : 4 * COLS, :] = wide[4 * MAIN : 4 * COLS, :].astype(BF16)

    loads[3].wait()
    widen(kraw, wide_k)
    loads[4].wait()
    widen(vraw, wide_v)

    def prep_kv(u, carry):
        o, k = u // KV, u % KV
        for a in range(0, DEEP, DIM):
            if a + DIM < MAIN:
                x = wide_k[rows_of(o, k, a, DIM), :]
                v = wide_v[rows_of(o, k, a, DIM), :]
                n = DIM
            else:
                n = PADDED - a
                fill = jnp.zeros((DIM - n, DIM), F32)
                x = [wide_k[rows_of(o, k, a, MAIN - a), :], tail_of(wide_k, o, k), fill]
                v = [wide_v[rows_of(o, k, a, MAIN - a), :], tail_of(wide_v, o, k), fill]
                x, v = jnp.concatenate(x, axis=0), jnp.concatenate(v, axis=0)
            unit, _ = unit_of(x)
            hat = unit * kgain_ref[...]
            khat[o, k, a : a + n, :] = hat.astype(BF16)[:n]
            vpad[o, k, a : a + n, :] = v.astype(BF16)[:n]
            turned_k[o, k, :, a : a + DIM] = hat.T.astype(BF16)
            turned_v[o, k, :, a : a + DIM] = v.T.astype(BF16)
        return carry

    lax.fori_loop(0, 2 * KV, prep_kv, 0)

    @pl.when(outer)
    def _():
        sends[1].start()

    sends[2].start()
    sends[1].wait_send()
    sends[3].start()

    def chosen(buf, o, count, lanes):
        x = buf[0, :, lanes].astype(F32)
        for r in range(1, count):
            x = jnp.where(rels[o] == r, buf[r, :, lanes].astype(F32), x)
        return x

    def prep_q(o, count):
        def body(hc, carry):
            x = chosen(qbuf, o, count, pl.ds(pl.multiple_of(hc * ROWS, ROWS), ROWS))
            k, c = hc // (PER // 2), hc % (PER // 2)
            for h in range(2):
                unit, _ = unit_of(x[:, h * DIM : (h + 1) * DIM])
                hat = unit * qgain_ref[...]
                at = pl.ds(pl.multiple_of(c * ROWS + h * TEXT, TEXT), TEXT)
                qh[o, k, at, :] = hat.astype(BF16)
                qhT[o, k, :, at] = hat.T.astype(BF16)
            return carry

        lax.fori_loop(0, CHUNKS, body, 0)

    def put_rows(ref, o, k, row):
        for h in range(PER):
            ref[o, k * PER + h : k * PER + h + 1, :] = row[:, h * TEXT : (h + 1) * TEXT]

    def get_rows(ref, o, k):
        rows = ref[o, pl.ds(pl.multiple_of(k * PER, PER), PER), :]
        return jnp.concatenate([rows[h : h + 1] for h in range(PER)], axis=1)

    tail_mask = lax.broadcasted_iota(jnp.int32, (PADDED - MAIN, SPAN), 0) == 0
    STEP = 160

    def score_step(u, at, n, top):
        o, k = u // KV, u % KV
        s = dot(khat[o, k, at, :], qhT[o, k])
        if n < STEP:
            s = jnp.where(tail_mask, s, -jnp.inf)
        e_ref[u, at, :] = s
        return jnp.maximum(top, fold(s, jnp.max))

    def exp_step(u, at, top, total):
        e = jnp.exp2((e_ref[u, at, :] - top) * (SCALE * LOG2E))
        e_ref[u, at, :] = e
        return total + fold(e, jnp.sum)

    lowest = jnp.full((8, SPAN), -jnp.inf, F32)
    nothing = jnp.zeros((8, SPAN), F32)

    def sweep(now, ahead, top):
        def body(i, carry):
            total, high = carry
            at = pl.ds(pl.multiple_of(i * STEP, STEP), STEP)
            if ahead is not None:
                high = score_step(ahead, at, STEP, high)
            if now is not None:
                total = exp_step(now, at, top, total)
            return total, high

        total, high = lax.fori_loop(0, MAIN // STEP, body, (nothing, lowest))
        at = slice(MAIN, PADDED)
        if ahead is not None:
            high = score_step(ahead, at, PADDED - MAIN, high)
        if now is not None:
            total = exp_step(now, at, top, total)
        return jnp.sum(total, axis=0, keepdims=True), jnp.max(high, axis=0, keepdims=True)

    def weigh(u, top, total):
        o, k = u // KV, u % KV
        inverse = 1.0 / total
        out = None
        for a in range(0, PADDED, 2 * DIM):
            n = min(2 * DIM, PADDED - a)
            p = (e_ref[u, a : a + n, :] * inverse).astype(BF16)
            if n < 2 * DIM:
                p = jnp.concatenate([p, jnp.zeros((DEEP - a - n, SPAN), BF16)], axis=0)
            part = dot(turned_v[o, k, :, a : a + p.shape[0]], p)
            out = part if out is None else out + part
        o_ref[o, k] = out
        put_rows(m_ref, o, k, top * SCALE)
        put_rows(w_ref, o, k, top * SCALE + jnp.log(total))

    loads[1].wait()
    arrived(0, qbuf, 1)

    @pl.when(inner)
    def _():
        arrived(0, qbuf, 2)

    prep_q(0, 3)
    _, top = sweep(None, 0, None)
    total, ahead = sweep(0, 1, top)
    weigh(0, top, total)
    top = ahead

    @pl.when(inner)
    def _():
        arrived(0, qbuf, 3)

    prep_q(1, 4)
    for u in range(1, 2 * KV):
        total, ahead = sweep(u, u + 1 if u + 1 < 2 * KV else None, top)
        weigh(u, top, total)
        top = ahead

    loads[2].wait()
    arrived(1, gbuf, 1)

    @pl.when(inner)
    def _():
        arrived(1, gbuf, 2)
        arrived(1, gbuf, 3)

    for o in range(2):

        def delta(hc, carry):
            x = chosen(gbuf, o, 3 + o, pl.ds(pl.multiple_of(hc * ROWS, ROWS), ROWS))
            k, c = hc // (PER // 2), hc % (PER // 2)
            out = o_ref[o, k, :, pl.ds(pl.multiple_of(c * ROWS, ROWS), ROWS)]
            for h in range(2):
                part = slice(h * TEXT, (h + 1) * TEXT)
                put = pl.ds(pl.multiple_of(c * ROWS + h * TEXT, TEXT), TEXT)
                raw = x[:, part]
                turned_raw = raw.T
                grad = (gate * turned_raw).astype(BF16)
                gs[o, k, put, :] = (gate * raw).astype(BF16)
                gsT[o, k, :, put] = grad
                at = pl.ds(2 * hc + h, 1)
                d_ref[o, at, :] = jnp.sum(out[:, part] * grad.astype(F32), axis=0, keepdims=True)
                gam_ref[o, at, :] = jnp.sum(out[:, part] * turned_raw, axis=0, keepdims=True)
            return carry

        lax.fori_loop(0, CHUNKS, delta, 0)
        saw = jnp.broadcast_to(seen[o], (HEADS, TEXT)) > 0.0
        stats[j, slot_of(o), 0] = jnp.where(saw, w_ref[o], NEGATIVE)
        stats[j, slot_of(o), 1] = jnp.where(saw, d_ref[o], 0.0)

    swaps = []
    for step in range(1, GROUP):
        swaps.append(
            remote(
                stats.at[j], stats.at[j], stat_send.at[step - 1], stat_recv.at[j],
                base + (j + step) % GROUP,
            )
        )
    for c in swaps:
        c.start()
    for step in range(1, GROUP):
        other = (j + step) % GROUP
        remote(stats.at[j], stats.at[other], stat_send.at[0], stat_recv.at[other], near).wait_recv()

    gate_sum = jnp.zeros((HEADS, TEXT), F32)
    for o in range(2):
        mine = [img_ref[2 * base + i] - base == docs[o] for i in range(2 * GROUP)]
        lses = [
            jnp.where(mine[i], stats[i // 2, i % 2, 0], 2.0 * NEGATIVE) for i in range(2 * GROUP)
        ]
        top = functools.reduce(jnp.maximum, lses)
        terms = [jnp.exp(x - top) for x in lses]
        total = functools.reduce(jnp.add, terms)
        weighted = [
            t * jnp.where(mine[i], stats[i // 2, i % 2, 1], 0.0) for i, t in enumerate(terms)
        ]
        saw = jnp.broadcast_to(seen[o], (HEADS, TEXT)) > 0.0
        own = jnp.where(saw, w_ref[o], NEGATIVE)
        d_ref[o] = functools.reduce(jnp.add, weighted) / total
        f_ref[o] = jnp.where(saw, jnp.exp(m_ref[o] - (top + jnp.log(total))), 0.0)
        w_ref[o] = jnp.where(saw, jnp.exp(own - top) / total, 0.0)
        gate_sum = gate_sum + w_ref[o] * gam_ref[o]

    def share(pair, own_b, near_b, far_b, k, lanes):
        def total(r):
            a = jnp.where(rels[0] == r, pair[0], 0.0)
            return a + jnp.where(rels[1] == r, pair[1], 0.0)

        own_b[k, :, lanes] = total(0)
        near_b[k, :, lanes] = total(1)
        far_b[0, k, :, lanes] = total(2).astype(BF16)
        far_b[1, k, :, lanes] = total(3).astype(BF16)

    def returns(which, k, near_b, far_b, rnear_b, rfar_b):
        one = remote(
            near_b.at[k], rnear_b.at[k], ret_send.at[which, k, 0], ret_recv.at[which, k, 0], near
        )
        two = [
            remote(
                far_b.at[r, k], rfar_b.at[k], ret_send.at[which, k, 1 + r],
                ret_recv.at[which, k, 1], base + jnp.where(j == 1, 2 + r, 1 - r),
            )
            for r in range(2)
        ]
        return one, two

    def start_returns(*args):
        one, two = returns(*args)
        one.start()

        @pl.when(inner)
        def _():
            for c in two:
                c.start()

    def finish_sends(*args):
        one, two = returns(*args)
        one.wait_send()

        @pl.when(inner)
        def _():
            for c in two:
                c.wait_send()

    def wait_returns(*args):
        one, two = returns(*args)
        one.wait_recv()
        two[0].wait_recv()

    o_args = (near_o, far_o, rnear_o, rfar_o)
    q_args = (near_q, far_q, rnear_q, rfar_q)

    def give_out(k, carry):
        def body(c, carry):
            hc = k * (PER // 2) + c
            pair = []
            for o in range(2):
                w = [w_ref[o, pl.ds(2 * hc + h, 1), :] for h in range(2)]
                x = o_ref[o, k, :, pl.ds(pl.multiple_of(c * ROWS, ROWS), ROWS)]
                x = x * jnp.concatenate(w, axis=1)
                pair.append(jnp.concatenate([x[:, :TEXT].T, x[:, TEXT:].T], axis=1))
            share(pair, own_o, near_o, far_o, k, pl.ds(pl.multiple_of(c * ROWS, ROWS), ROWS))
            return carry

        lax.fori_loop(0, PER // 2, body, 0)
        start_returns(0, k, *o_args)
        return carry

    lax.fori_loop(0, KV, give_out, 0)

    def backward(k, sums):
        kgain_sum, qgain_sum = sums

        def per_slot(o, kgain_sum):
            factor = get_rows(f_ref, o, k)
            delta = get_rows(d_ref, o, k)
            for a in range(0, PADDED, 2 * DIM):
                n = min(2 * DIM, PADDED - a)
                dp = dot(vpad[o, k, a : a + n, :], gsT[o, k])
                p = e_ref[2 * o + k, a : a + n, :] * factor
                ds = (p * (dp - delta)).astype(BF16)
                value = dot(p.astype(BF16), gs[o, k])
                up = dot(ds, qh[o, k]) * SCALE
                if n < 2 * DIM:
                    ds = jnp.concatenate([ds, jnp.zeros((DEEP - a - n, SPAN), BF16)], axis=0)
                part = dot(turned_k[o, k, :, a : a + ds.shape[0]], ds)
                if a == 0:
                    x_acc[...] = part
                else:
                    x_acc[...] += part
                whole = min(n, MAIN - a)
                x = wide_k[rows_of(o, k, a, whole), :]
                if whole < n:
                    x = jnp.concatenate([x, tail_of(wide_k, o, k)], axis=0)
                unit, inverse = unit_of(x)
                scaled = up * kgain_ref[...]
                back = inverse * (scaled - unit * jnp.mean(scaled * unit, axis=1, keepdims=True))
                kgain_sum = kgain_sum + fold(up * unit, jnp.sum)
                wide_k[rows_of(o, k, a, whole), :] = back[:whole]
                wide_v[rows_of(o, k, a, whole), :] = value[:whole]
                if whole < n:
                    at = pl.ds(4 * MAIN + 2 * k + slot_of(o), 1)
                    wide_k[at, :] = back[whole : whole + 1]
                    wide_v[at, :] = value[whole : whole + 1]
            for c in range(PER // 2):
                dq_ref[o, c] = jnp.concatenate(
                    [x_acc[:, c * ROWS + h * TEXT : c * ROWS + (h + 1) * TEXT].T for h in range(2)], axis=1
                )
            return kgain_sum

        kgain_sum = lax.fori_loop(0, 2, per_slot, kgain_sum)

        def body(c, qgain_sum):
            pair = [dq_ref[0, c], dq_ref[1, c]]
            share(pair, own_q, near_q, far_q, k, pl.ds(pl.multiple_of(c * ROWS, ROWS), ROWS))
            full = pl.ds(pl.multiple_of(k * PER * DIM + c * ROWS, ROWS), ROWS)
            for o in range(2):
                x = chosen(qbuf, o, 3 + o, full)
                for h in range(2):
                    part = slice(h * DIM, (h + 1) * DIM)
                    unit, _ = unit_of(x[:, part])
                    qgain_sum = qgain_sum + fold(pair[o][:, part] * unit, jnp.sum)
            return qgain_sum

        qgain_sum = lax.fori_loop(0, PER // 2, body, qgain_sum)
        start_returns(1, k, *q_args)
        return kgain_sum, qgain_sum

    zero = jnp.zeros((8, DIM), F32)
    kgain_sum, qgain_sum = lax.fori_loop(0, KV, backward, (zero, zero))

    row = lax.broadcasted_iota(jnp.int32, (8, DIM), 0)
    gate_total = jnp.sum(jnp.sum(gate_sum, axis=0, keepdims=True), axis=1, keepdims=True)
    part = jnp.where(
        row == 0,
        jnp.sum(qgain_sum, axis=0, keepdims=True) * SCALE,
        jnp.where(
            row == 1,
            jnp.sum(kgain_sum, axis=0, keepdims=True),
            (1.0 - gate * gate) * gate_total,
        ),
    )

    def stage_copies(n):
        axis, stride, count, mine, low = place(stages[n])
        buf = sum_bufs[n]
        out, come = [], []
        for step in range(1, count):
            other = (mine + step) % count
            for at, to, found in ((mine, out, step), (other, come, 0)):
                to.append(
                    pltpu.make_async_remote_copy(
                        src_ref=buf.at[at], dst_ref=buf.at[at], send_sem=sum_send.at[n, found],
                        recv_sem=sum_recv.at[n, at], device_id={axis: low + stride * other},
                        device_id_type=MESH,
                    )
                )
        return out, come

    def stage_start(n, value):
        sum_bufs[n][place(stages[n])[3]] = value
        for c in stage_copies(n)[0]:
            c.start()

    def stage_end(n):
        for c in stage_copies(n)[1]:
            c.wait_recv()
        value = sum_bufs[n][0]
        for i in range(1, stages[n][2]):
            value = value + sum_bufs[n][i]
        return value

    stage_start(0, part)

    narrow(wide_k, kraw)
    narrow(wide_v, vraw)
    outs = [
        pltpu.make_async_copy(kraw, dk_hbm, out_sem.at[0]),
        pltpu.make_async_copy(vraw, dv_hbm, out_sem.at[1]),
    ]
    for c in outs:
        c.start()
    part = stage_end(0)
    if len(stages) > 1:
        stage_start(1, part)

    for k in range(KV):
        wait_returns(0, k, *o_args)

    def attend(k, carry):
        for c in range(PER):
            lanes = slice(c * DIM, (c + 1) * DIM)
            full = pl.ds(pl.multiple_of(k * PER * DIM + c * DIM, DIM), DIM)
            merged = own_o[k, :, lanes] + rnear_o[k, :, lanes] + rfar_o[k, :, lanes].astype(F32)
            att_v[:, full] = (gate * merged).astype(BF16)
        return carry

    lax.fori_loop(0, KV, attend, 0)
    out_att = pltpu.make_async_copy(att_v, att_hbm.at[0], out_sem.at[4])
    out_att.start()
    if len(stages) > 1:
        part = stage_end(1)
    if len(stages) > 2:
        stage_start(2, part)

    for k in range(KV):
        wait_returns(1, k, *q_args)

    def finish(k, carry):
        for c in range(PER):
            lanes = slice(c * DIM, (c + 1) * DIM)
            full = pl.ds(pl.multiple_of(k * PER * DIM + c * DIM, DIM), DIM)
            hat = own_q[k, :, lanes] + rnear_q[k, :, lanes] + rfar_q[k, :, lanes].astype(F32)
            hat = hat * SCALE
            unit, inverse = unit_of(qbuf[0, :, full].astype(F32))
            scaled = hat * qgain_ref[...]
            back = inverse * (scaled - unit * jnp.mean(scaled * unit, axis=1, keepdims=True))
            dq_v[:, full] = back.astype(BF16)
        return carry

    lax.fori_loop(0, KV, finish, 0)
    out_dq = pltpu.make_async_copy(dq_v, dq_hbm.at[0], out_sem.at[5])
    out_dq.start()

    if len(stages) > 2:
        part = stage_end(2)
    qg_out[...] = part[0:1]
    kg_out[...] = part[1:2]
    gate_out[...] = part[2:3, 0:1]
    for n in range(len(stages)):
        for c in stage_copies(n)[0]:
            c.wait_send()
    for c in (sends[0], sends[2], sends[3]):
        c.wait_send()
    for c in swaps:
        c.wait_send()
    for k in range(KV):
        finish_sends(0, k, *o_args)
        finish_sends(1, k, *q_args)
    for c in outs:
        c.wait()
    out_att.wait()
    out_dq.wait()


def run_main(stages, img, gate, qgain, kgain, text_mask, q, g, kk, vv):
    vm = pltpu.VMEM
    dma = pltpu.SemaphoreType.DMA
    half = (KV, TEXT, PER * DIM)
    slots = text_mask.shape[0]
    scratch = [
        vm((slots, 8, TEXT), jnp.int32),
        vm((4, TEXT, HEADS * DIM), BF16),
        vm((4, TEXT, HEADS * DIM), BF16),
        vm((COLS, 4, DIM), BF16),
        vm((COLS, 4, DIM), BF16),
        vm((4 * PADDED, DIM), F32),
        vm((4 * PADDED, DIM), F32),
        vm((2, KV, PADDED, DIM), BF16),
        vm((2, KV, PADDED, DIM), BF16),
        vm((2, KV, DIM, DEEP), BF16),
        vm((2, KV, DIM, DEEP), BF16),
        vm((2, KV, SPAN, DIM), BF16),
        vm((2, KV, DIM, SPAN), BF16),
        vm((2, KV, SPAN, DIM), BF16),
        vm((2, KV, DIM, SPAN), BF16),
        vm((2 * KV, PADDED, SPAN), F32),
        vm((2, KV, DIM, SPAN), F32),
        vm((2, PER // 2, TEXT, ROWS), F32),
        vm((DIM, SPAN), F32),
        vm((2, HEADS, TEXT), F32),
        vm((2, HEADS, TEXT), F32),
        vm((2, HEADS, TEXT), F32),
        vm((2, HEADS, TEXT), F32),
        vm((2, HEADS, TEXT), F32),
        vm((GROUP, 2, 2, HEADS, TEXT), F32),
        vm(half, F32),
        vm(half, F32),
        vm((2,) + half, BF16),
        vm(half, F32),
        vm(half, F32),
        vm((2,) + half, BF16),
        vm(half, F32),
        vm(half, BF16),
        vm(half, F32),
        vm(half, BF16),
        vm((TEXT, HEADS * DIM), BF16),
        vm((TEXT, HEADS * DIM), BF16),
        dma((7,)),
        dma((4,)),
        dma((2, 4)),
        dma((3,)),
        dma((4,)),
        dma((2, KV, 3)),
        dma((2, KV, 2)),
        dma((6,)),
        dma((len(stages), max(s[2] for s in stages))),
        dma((len(stages), max(s[2] for s in stages))),
    ] + [vm((s[2], 8, DIM), F32) for s in stages]
    hbm = pl.BlockSpec(memory_space=pl.ANY)
    vmem = pl.BlockSpec(memory_space=pltpu.VMEM)
    return pl.pallas_call(
        functools.partial(main_kernel, stages),
        out_shape=(
            jax.ShapeDtypeStruct(q.shape, BF16),
            jax.ShapeDtypeStruct(q.shape, BF16),
            jax.ShapeDtypeStruct(kk.shape, BF16),
            jax.ShapeDtypeStruct(vv.shape, BF16),
            jax.ShapeDtypeStruct((1, DIM), F32),
            jax.ShapeDtypeStruct((1, DIM), F32),
            jax.ShapeDtypeStruct((1, 1), F32),
        ),
        in_specs=[pl.BlockSpec(memory_space=pltpu.SMEM), vmem, vmem, vmem] + [hbm] * 5,
        out_specs=(hbm, hbm, hbm, hbm, vmem, vmem, vmem),
        scratch_shapes=scratch,
        compiler_params=pltpu.CompilerParams(
            collective_id=0, has_side_effects=True, vmem_limit_bytes=64 * 1024 * 1024
        ),
    )(img, gate, qgain, kgain, text_mask, q, g, kk, vv)


def stages_of(sizes):
    low = min(8, sizes["dp"])
    out = [("dp", 1, low)]
    if sizes["heads"] > 1:
        out.append(("heads", 1, sizes["heads"]))
    if sizes["dp"] > low:
        out.append(("dp", low, sizes["dp"] // low))
    return out


def interleaved(x):
    x = x.transpose(1, 0, 2).reshape(COLS, 2, KV, DIM)
    return x.transpose(0, 2, 1, 3).reshape(COLS, 2 * KV, DIM)


def separated(x):
    return x.reshape(COLS, KV, 2, DIM).transpose(2, 0, 1, 3).reshape(2, COLS, KV * DIM)


def solution(mesh):
    sizes = dict(mesh.shape)

    def per_device(q, qgain, kk, vv, kgain, gate, img, text_mask, g):
        att, dq, dk, dv, qg, kg, gt = run_main(
            stages_of(sizes), img, gate.reshape(1, 1), qgain.reshape(1, DIM),
            kgain.reshape(1, DIM), text_mask.transpose(2, 0, 1), q, g, interleaved(kk),
            interleaved(vv),
        )
        return (
            att, dq, separated(dk), separated(dv), qg.reshape(DIM), kg.reshape(DIM), gt.reshape(1)
        )

    split = P("dp", None, "heads")
    return jax.shard_map(
        per_device,
        mesh=mesh,
        in_specs=(split, P(), split, split, P(), P(), P(), P(), split),
        out_specs=(split, split, split, split, P(), P(), P()),
        check_vma=False,
    )
```

time: 144 us -> 96.3 us (0.67)
  local copies, waits for them, and re-layouts: 32.9 us -> 8.1 us
  Pallas kernels: 108 us -> 84.6 us
    unnamed x23 -> x14, local copies, waits for them, and re-layouts: 32.9 us -> 8.1 us
    pallas_call x2 -> x1, Pallas kernels: 108 us -> 84.6 us  [run_main(): pl.pallas_call(functools.partial(main_kernel, stages), out_shape=(jax.Sha...]
where the time goes in v2:
time: 96.3 us; the launch traced here: 95.8 us
  Pallas kernels  84.6 us (88%)
  local copies, waits for them, and re-layouts  8.1 us (8%)
  between operations  3.12 us (3%)
    pallas_call x1, Pallas kernels, run_main(): pl.pallas_call(functools.partial(main_kernel, stages), out_shape=(jax.Sha...  84.6 us
    unnamed x14, local copies, waits for them, and re-layouts  8.1 us

profile of v2, /device:TPU:1, one launch (start us, length us, event | category | flops | bytes accessed | tf_op | source)
XLA Modules:
  0.0 95.8 jit_solution(10155512090096168802)
XLA Ops:
  1.3 84.6 %shard_map.144 = (bf16[1,128,2048]{2,1,0:T(8,128)(2,1)}, bf16[1,128,2048]{2,1,0:T(8,128)(2,1)}, bf16[1601,4,128]{2,1,0:T(4,128)(2,1)}, bf16[1601,4,128]{2,1,0:T(...) custom-call(s32[128]{0:T(128)} %img_ref.1, f32[1,1]{1,0:T(1,128)} %bitcast.31.gate_ref, ...), custom_call_target="tpu_custom_call" | custom-call | tf_op jit(solution)/shard_map/pallas_call | solution.py:744
  85.9 0.0 copy-start.1
  85.9 2.0 %copy.28 = bf16[1,128,2048]{2,1,0:T(8,128)(2,1)} copy(bf16[1,128,2048]{2,1,0:T(8,128)(2,1)} %get-tuple-element.28) | data formatting | bytes 1048576
  87.9 1.9 %copy.29 = bf16[1,128,2048]{2,1,0:T(8,128)(2,1)} copy(bf16[1,128,2048]{2,1,0:T(8,128)(2,1)} %get-tuple-element.29) | data formatting | bytes 1048576
  89.7 0.0 copy-done.1
  89.8 0.0 copy-start
  89.8 1.2 %copy.30 = bf16[2,1601,256]{2,0,1:T(2,128)(2,1)} copy(bf16[2,1601,256]{2,0,1:T(2,128)(2,1)S(1)} %bitcast.35) | data formatting | bytes 3278848
  90.9 0.9 copy-done
  91.8 0.0 copy-start.3
  91.8 0.0 copy-start.2
  91.8 1.2 %copy.31 = bf16[2,1601,256]{2,0,1:T(2,128)(2,1)} copy(bf16[2,1601,256]{2,0,1:T(2,128)(2,1)S(1)} %bitcast.34) | data formatting | bytes 3278848
  92.9 0.0 copy-done.3
  92.9 0.5 copy.32
  93.5 0.0 copy-done.2
  93.5 0.5 copy.33
Async XLA Ops:
  85.9 3.9 %copy-start.1 = (bf16[1601,4,128]{2,1,0:T(4,128)(2,1)S(1)}, bf16[1601,4,128]{2,1,0:T(4,128)(2,1)}, u32[]{:S(2)}) copy-start(bf16[1601,4,128]{2,1,0:T(4,128)(2,1)} %get-tuple-element.16) | copy-start | bytes 4918276
  89.8 2.0 %copy-start = (bf16[1601,4,128]{2,1,0:T(4,128)(2,1)S(1)}, bf16[1601,4,128]{2,1,0:T(4,128)(2,1)}, u32[]{:S(2)}) copy-start(bf16[1601,4,128]{2,1,0:T(4,128)(2,1)} %get-tuple-element.17) | copy-start | bytes 4918276
  91.8 1.2 %copy-start.3 = (f32[1,128]{1,0:T(1,128)S(1)}, f32[1,128]{1,0:T(1,128)}, u32[]{:S(2)}) copy-start(f32[1,128]{1,0:T(1,128)} %get-tuple-element.18) | copy-start | bytes 1540
  91.8 1.7 %copy-start.2 = (f32[1,128]{1,0:T(1,128)S(1)}, f32[1,128]{1,0:T(1,128)}, u32[]{:S(2)}) copy-start(f32[1,128]{1,0:T(1,128)} %get-tuple-element.19) | copy-start | bytes 1540

commit v3 on v2

--- a/solution.py
+++ b/solution.py
@@ -98,8 +98,6 @@
     rfar_o,
     rnear_q,
     rfar_q,
-    att_v,
-    dq_v,
     load_sem,
     send_sem,
     recv_sem,
@@ -155,21 +153,36 @@
             device_id={"dp": dev}, device_id_type=MESH,
         )
 
-    sends = [
-        remote(q_hbm.at[0], qbuf.at[1], send_sem.at[0], recv_sem.at[0, 1], near),
-        remote(q_hbm.at[0], qbuf.at[far_slot], send_sem.at[1], recv_sem.at[0, far_slot], far),
-        remote(g_hbm.at[0], gbuf.at[1], send_sem.at[2], recv_sem.at[1, 1], near),
-        remote(g_hbm.at[0], gbuf.at[far_slot], send_sem.at[3], recv_sem.at[1, far_slot], far),
-    ]
-    sends[0].start()
-
-    @pl.when(inner)
-    def _():
-        sends[1].start()
-
-    def arrived(which, buf, slot):
-        src = (q_hbm, g_hbm)[which]
-        remote(src.at[0], buf.at[slot], send_sem.at[0], recv_sem.at[which, slot], near).wait_recv()
+    def half_of(ref, k):
+        return ref.at[:, pl.ds(k * PER * DIM, PER * DIM)]
+
+    def q_send(slot, k, ss, dev):
+        return remote(
+            half_of(q_hbm.at[0], k), half_of(qbuf.at[slot], k), ss, recv_sem.at[k, slot], dev
+        )
+
+    def g_send(slot, ss, dev):
+        return remote(g_hbm.at[0], gbuf.at[slot], ss, recv_sem.at[2, slot], dev)
+
+    q_near = [q_send(1, k, send_sem.at[k], near) for k in range(KV)]
+    q_far = [q_send(far_slot, k, send_sem.at[2 + k], far) for k in range(KV)]
+    g_near = g_send(1, send_sem.at[4], near)
+    g_far = g_send(far_slot, send_sem.at[5], far)
+
+    def start_where(condition, *copies):
+        @pl.when(condition)
+        def _():
+            for c in copies:
+                c.start()
+
+    q_near[0].start()
+    start_where(inner, q_far[0])
+
+    def q_arrived(slot, k):
+        q_send(slot, k, send_sem.at[0], near).wait_recv()
+
+    def g_arrived(slot):
+        g_send(slot, send_sem.at[0], near).wait_recv()
 
     docs, rels, ranks = [], [], []
     for o in range(2):
@@ -241,6 +254,9 @@
 
     loads[3].wait()
     widen(kraw, wide_k)
+
+    q_near[1].start()
+    start_where(inner, q_far[1])
     loads[4].wait()
     widen(vraw, wide_v)
 
@@ -267,13 +283,8 @@
 
     lax.fori_loop(0, 2 * KV, prep_kv, 0)
 
-    @pl.when(outer)
-    def _():
-        sends[1].start()
-
-    sends[2].start()
-    sends[1].wait_send()
-    sends[3].start()
+    start_where(outer, q_far[0])
+    g_near.start()
 
     def chosen(buf, o, count, lanes):
         x = buf[0, :, lanes].astype(F32)
@@ -281,10 +292,10 @@
             x = jnp.where(rels[o] == r, buf[r, :, lanes].astype(F32), x)
         return x
 
-    def prep_q(o, count):
-        def body(hc, carry):
+    def prep_q(o, k, count):
+        def body(c, carry):
+            hc = k * (PER // 2) + c
             x = chosen(qbuf, o, count, pl.ds(pl.multiple_of(hc * ROWS, ROWS), ROWS))
-            k, c = hc // (PER // 2), hc % (PER // 2)
             for h in range(2):
                 unit, _ = unit_of(x[:, h * DIM : (h + 1) * DIM])
                 hat = unit * qgain_ref[...]
@@ -293,7 +304,7 @@
                 qhT[o, k, :, at] = hat.T.astype(BF16)
             return carry
 
-        lax.fori_loop(0, CHUNKS, body, 0)
+        lax.fori_loop(0, PER // 2, body, 0)
 
     def put_rows(ref, o, k, row):
         for h in range(PER):
@@ -304,7 +315,7 @@
         return jnp.concatenate([rows[h : h + 1] for h in range(PER)], axis=1)
 
     tail_mask = lax.broadcasted_iota(jnp.int32, (PADDED - MAIN, SPAN), 0) == 0
-    STEP = 160
+    STEP = 400
 
     def score_step(u, at, n, top):
         o, k = u // KV, u % KV
@@ -355,36 +366,49 @@
         put_rows(m_ref, o, k, top * SCALE)
         put_rows(w_ref, o, k, top * SCALE + jnp.log(total))
 
+    def ready_q(o, k):
+        if o == 0:
+            q_arrived(1, k)
+
+        @pl.when(inner)
+        def _():
+            q_arrived(2 + o, k)
+
+        prep_q(o, k, 3 + o)
+
     loads[1].wait()
-    arrived(0, qbuf, 1)
+    ready_q(0, 0)
+    _, top = sweep(None, 0, None)
+    start_where(outer, q_far[1])
+    ready_q(0, 1)
 
     @pl.when(inner)
     def _():
-        arrived(0, qbuf, 2)
-
-    prep_q(0, 3)
-    _, top = sweep(None, 0, None)
-    total, ahead = sweep(0, 1, top)
-    weigh(0, top, total)
-    top = ahead
-
-    @pl.when(inner)
-    def _():
-        arrived(0, qbuf, 3)
-
-    prep_q(1, 4)
-    for u in range(1, 2 * KV):
+        for c in q_far:
+            c.wait_send()
+        g_far.start()
+
+    for u in range(2 * KV):
         total, ahead = sweep(u, u + 1 if u + 1 < 2 * KV else None, top)
         weigh(u, top, total)
         top = ahead
+        if u + 2 < 2 * KV:
+            ready_q((u + 2) // KV, (u + 2) % KV)
+        if u == 0:
+
+            @pl.when(outer)
+            def _():
+                for c in q_far:
+                    c.wait_send()
+                g_far.start()
 
     loads[2].wait()
-    arrived(1, gbuf, 1)
+    g_arrived(1)
 
     @pl.when(inner)
     def _():
-        arrived(1, gbuf, 2)
-        arrived(1, gbuf, 3)
+        g_arrived(2)
+        g_arrived(3)
 
     for o in range(2):
 
@@ -513,7 +537,7 @@
     def backward(k, sums):
         kgain_sum, qgain_sum = sums
 
-        def per_slot(o, kgain_sum):
+        def per_slot(o, carry):
             factor = get_rows(f_ref, o, k)
             delta = get_rows(d_ref, o, k)
             for a in range(0, PADDED, 2 * DIM):
@@ -522,7 +546,7 @@
                 p = e_ref[2 * o + k, a : a + n, :] * factor
                 ds = (p * (dp - delta)).astype(BF16)
                 value = dot(p.astype(BF16), gs[o, k])
-                up = dot(ds, qh[o, k]) * SCALE
+                e_ref[2 * o + k, a : a + n, :DIM] = dot(ds, qh[o, k])
                 if n < 2 * DIM:
                     ds = jnp.concatenate([ds, jnp.zeros((DEEP - a - n, SPAN), BF16)], axis=0)
                 part = dot(turned_k[o, k, :, a : a + ds.shape[0]], ds)
@@ -531,26 +555,16 @@
                 else:
                     x_acc[...] += part
                 whole = min(n, MAIN - a)
-                x = wide_k[rows_of(o, k, a, whole), :]
-                if whole < n:
-                    x = jnp.concatenate([x, tail_of(wide_k, o, k)], axis=0)
-                unit, inverse = unit_of(x)
-                scaled = up * kgain_ref[...]
-                back = inverse * (scaled - unit * jnp.mean(scaled * unit, axis=1, keepdims=True))
-                kgain_sum = kgain_sum + fold(up * unit, jnp.sum)
-                wide_k[rows_of(o, k, a, whole), :] = back[:whole]
                 wide_v[rows_of(o, k, a, whole), :] = value[:whole]
                 if whole < n:
-                    at = pl.ds(4 * MAIN + 2 * k + slot_of(o), 1)
-                    wide_k[at, :] = back[whole : whole + 1]
-                    wide_v[at, :] = value[whole : whole + 1]
+                    wide_v[pl.ds(4 * MAIN + 2 * k + slot_of(o), 1), :] = value[whole : whole + 1]
             for c in range(PER // 2):
                 dq_ref[o, c] = jnp.concatenate(
                     [x_acc[:, c * ROWS + h * TEXT : c * ROWS + (h + 1) * TEXT].T for h in range(2)], axis=1
                 )
-            return kgain_sum
-
-        kgain_sum = lax.fori_loop(0, 2, per_slot, kgain_sum)
+            return carry
+
+        lax.fori_loop(0, 2, per_slot, 0)
 
         def body(c, qgain_sum):
             pair = [dq_ref[0, c], dq_ref[1, c]]
@@ -566,7 +580,26 @@
 
         qgain_sum = lax.fori_loop(0, PER // 2, body, qgain_sum)
         start_returns(1, k, *q_args)
-        return kgain_sum, qgain_sum
+
+        def norm_back(o, kgain_sum):
+            def key_step(x, up, kgain_sum):
+                up = up * SCALE
+                unit, inverse = unit_of(x)
+                scaled = up * kgain_ref[...]
+                back = inverse * (scaled - unit * jnp.mean(scaled * unit, axis=1, keepdims=True))
+                return back, kgain_sum + fold(up * unit, jnp.sum)
+
+            for a in range(0, MAIN, STEP):
+                at = rows_of(o, k, a, STEP)
+                back, kgain_sum = key_step(wide_k[at, :], e_ref[2 * o + k, a : a + STEP, :DIM], kgain_sum)
+                wide_k[at, :] = back
+            back, kgain_sum = key_step(
+                tail_of(wide_k, o, k), e_ref[2 * o + k, MAIN:PADDED, :DIM], kgain_sum
+            )
+            wide_k[pl.ds(4 * MAIN + 2 * k + slot_of(o), 1), :] = back[:1]
+            return kgain_sum
+
+        return lax.fori_loop(0, 2, norm_back, kgain_sum), qgain_sum
 
     zero = jnp.zeros((8, DIM), F32)
     kgain_sum, qgain_sum = lax.fori_loop(0, KV, backward, (zero, zero))
@@ -614,14 +647,14 @@
 
     stage_start(0, part)
 
-    narrow(wide_k, kraw)
-    narrow(wide_v, vraw)
     outs = [
         pltpu.make_async_copy(kraw, dk_hbm, out_sem.at[0]),
         pltpu.make_async_copy(vraw, dv_hbm, out_sem.at[1]),
     ]
-    for c in outs:
-        c.start()
+    narrow(wide_k, kraw)
+    outs[0].start()
+    narrow(wide_v, vraw)
+    outs[1].start()
     part = stage_end(0)
     if len(stages) > 1:
         stage_start(1, part)
@@ -634,11 +667,11 @@
             lanes = slice(c * DIM, (c + 1) * DIM)
             full = pl.ds(pl.multiple_of(k * PER * DIM + c * DIM, DIM), DIM)
             merged = own_o[k, :, lanes] + rnear_o[k, :, lanes] + rfar_o[k, :, lanes].astype(F32)
-            att_v[:, full] = (gate * merged).astype(BF16)
+            gbuf[0, :, full] = (gate * merged).astype(BF16)
         return carry
 
     lax.fori_loop(0, KV, attend, 0)
-    out_att = pltpu.make_async_copy(att_v, att_hbm.at[0], out_sem.at[4])
+    out_att = pltpu.make_async_copy(gbuf.at[0], att_hbm.at[0], out_sem.at[4])
     out_att.start()
     if len(stages) > 1:
         part = stage_end(1)
@@ -657,11 +690,11 @@
             unit, inverse = unit_of(qbuf[0, :, full].astype(F32))
             scaled = hat * qgain_ref[...]
             back = inverse * (scaled - unit * jnp.mean(scaled * unit, axis=1, keepdims=True))
-            dq_v[:, full] = back.astype(BF16)
+            qbuf[0, :, full] = back.astype(BF16)
         return carry
 
     lax.fori_loop(0, KV, finish, 0)
-    out_dq = pltpu.make_async_copy(dq_v, dq_hbm.at[0], out_sem.at[5])
+    out_dq = pltpu.make_async_copy(qbuf.at[0], dq_hbm.at[0], out_sem.at[5])
     out_dq.start()
 
     if len(stages) > 2:
@@ -672,7 +705,7 @@
     for n in range(len(stages)):
         for c in stage_copies(n)[0]:
             c.wait_send()
-    for c in (sends[0], sends[2], sends[3]):
+    for c in (*q_near, g_near, g_far):
         c.wait_send()
     for c in swaps:
         c.wait_send()
@@ -726,11 +759,9 @@
         vm(half, BF16),
         vm(half, F32),
         vm(half, BF16),
-        vm((TEXT, HEADS * DIM), BF16),
-        vm((TEXT, HEADS * DIM), BF16),
         dma((7,)),
-        dma((4,)),
-        dma((2, 4)),
+        dma((6,)),
+        dma((3, 4)),
         dma((3,)),
         dma((4,)),
         dma((2, KV, 3)),
@@ -771,6 +802,47 @@
     return out
 
 
+PIECES = 4
+
+
+def copy_kernel(count, *refs):
+    stage = refs[2 * count : 3 * count]
+    come, leave = refs[3 * count :]
+    pairs = []
+    for i in range(count):
+        rows = refs[i].shape[0]
+        size = -(-rows // PIECES)
+        for n, a in enumerate(range(0, rows, size)):
+            at = pl.ds(a, min(size, rows - a))
+            pairs.append(
+                (
+                    pltpu.make_async_copy(refs[i].at[at], stage[i].at[at], come.at[i, n]),
+                    pltpu.make_async_copy(stage[i].at[at], refs[count + i].at[at], leave.at[i, n]),
+                )
+            )
+    for first, _ in pairs:
+        first.start()
+    for first, second in pairs:
+        first.wait()
+        second.start()
+    for _, second in pairs:
+        second.wait()
+
+
+def settled(*arrays):
+    hbm = pl.BlockSpec(memory_space=pl.ANY)
+    count = len(arrays)
+    return pl.pallas_call(
+        functools.partial(copy_kernel, count),
+        out_shape=tuple(jax.ShapeDtypeStruct(a.shape, a.dtype) for a in arrays),
+        in_specs=[hbm] * count,
+        out_specs=(hbm,) * count,
+        scratch_shapes=[pltpu.VMEM(a.shape, a.dtype) for a in arrays]
+        + [pltpu.SemaphoreType.DMA((count, PIECES))] * 2,
+        compiler_params=pltpu.CompilerParams(vmem_limit_bytes=64 * 1024 * 1024),
+    )(*arrays)
+
+
 def interleaved(x):
     x = x.transpose(1, 0, 2).reshape(COLS, 2, KV, DIM)
     return x.transpose(0, 2, 1, 3).reshape(COLS, 2 * KV, DIM)
@@ -784,11 +856,12 @@
     sizes = dict(mesh.shape)
 
     def per_device(q, qgain, kk, vv, kgain, gate, img, text_mask, g):
-        att, dq, dk, dv, qg, kg, gt = run_main(
+        found = run_main(
             stages_of(sizes), img, gate.reshape(1, 1), qgain.reshape(1, DIM),
             kgain.reshape(1, DIM), text_mask.transpose(2, 0, 1), q, g, interleaved(kk),
             interleaved(vv),
         )
+        att, dq, dk, dv, qg, kg, gt = settled(*found)
         return (
             att, dq, separated(dk), separated(dv), qg.reshape(DIM), kg.reshape(DIM), gt.reshape(1)
         )

time: 96.3 us -> 84.4 us (0.88)
  local copies, waits for them, and re-layouts: 8.1 us -> 0 us
  between operations: 3.12 us -> 1.29 us
  Pallas kernels: 84.6 us -> 83 us
    unnamed x14 -> x0, local copies, waits for them, and re-layouts: 8.1 us -> none
    pallas_call x1, Pallas kernels: 84.6 us -> 78.3 us  [run_main(): pl.pallas_call(functools.partial(main_kernel, stages), out_shape=(jax.Sha...]
    pallas_call x0 -> x1, Pallas kernels: none -> 4.7 us  [settled(): pl.pallas_call(functools.partial(copy_kernel, count), out_shape=tuple((ja...]
where the time goes in v3:
time: 84.4 us; the launch traced here: 84.3 us
  Pallas kernels  83 us (98%)
  between operations  1.29 us (2%)
    pallas_call x1, Pallas kernels, run_main(): pl.pallas_call(functools.partial(main_kernel, stages), out_shape=(jax.Sha...  78.3 us
    pallas_call x1, Pallas kernels, settled(): pl.pallas_call(functools.partial(copy_kernel, count), out_shape=tuple((ja...  4.7 us

profile of v3, /device:TPU:1, one launch (start us, length us, event | category | flops | bytes accessed | tf_op | source)
XLA Modules:
  0.0 84.3 jit_solution(656343834661028375)
XLA Ops:
  1.3 78.3 %shard_map.144 = (bf16[1,128,2048]{2,1,0:T(8,128)(2,1)}, bf16[1,128,2048]{2,1,0:T(8,128)(2,1)}, bf16[1601,4,128]{2,1,0:T(4,128)(2,1)}, bf16[1601,4,128]{2,1,0:T(...) custom-call(s32[128]{0:T(128)} %img_ref.1, f32[1,1]{1,0:T(1,128)} %bitcast.31.gate_ref, ...), custom_call_target="tpu_custom_call" | custom-call | tf_op jit(solution)/shard_map/pallas_call | solution.py:775
  79.6 4.7 %shard_map.145 = (bf16[1,128,2048]{2,1,0:T(8,128)(2,1)}, bf16[1,128,2048]{2,1,0:T(8,128)(2,1)}, bf16[1601,4,128]{2,1,0:T(4,128)(2,1)}, bf16[1601,4,128]{2,1,0:T(...) custom-call(bf16[1,128,2048]{2,1,0:T(8,128)(2,1)} %get-tuple-element.21.refs_0_, ...), custom_call_target="tpu_custom_call" | custom-call | tf_op jit(solution)/shard_map/pallas_call | solution.py:835

commit v4 on v3

--- a/solution.py
+++ b/solution.py
@@ -32,6 +32,10 @@
 
 def dot(a, b):
     return jnp.dot(a, b, preferred_element_type=F32)
+
+
+def crossed(a, b):
+    return lax.dot_general(a, b, (((1,), (1,)), ((), ())), preferred_element_type=F32)
 
 
 def fold(x, op):
@@ -87,6 +91,8 @@
     d_ref,
     w_ref,
     gam_ref,
+    lw_ref,
+    wt_ref,
     stats,
     own_o,
     near_o,
@@ -304,7 +310,7 @@
                 qhT[o, k, :, at] = hat.T.astype(BF16)
             return carry
 
-        lax.fori_loop(0, PER // 2, body, 0)
+        lax.fori_loop(0, PER // 2, body, 0, unroll=2)
 
     def put_rows(ref, o, k, row):
         for h in range(PER):
@@ -382,11 +388,7 @@
     start_where(outer, q_far[1])
     ready_q(0, 1)
 
-    @pl.when(inner)
-    def _():
-        for c in q_far:
-            c.wait_send()
-        g_far.start()
+    g_far.start()
 
     for u in range(2 * KV):
         total, ahead = sweep(u, u + 1 if u + 1 < 2 * KV else None, top)
@@ -394,14 +396,6 @@
         top = ahead
         if u + 2 < 2 * KV:
             ready_q((u + 2) // KV, (u + 2) % KV)
-        if u == 0:
-
-            @pl.when(outer)
-            def _():
-                for c in q_far:
-                    c.wait_send()
-                g_far.start()
-
     loads[2].wait()
     g_arrived(1)
 
@@ -429,7 +423,7 @@
                 gam_ref[o, at, :] = jnp.sum(out[:, part] * turned_raw, axis=0, keepdims=True)
             return carry
 
-        lax.fori_loop(0, CHUNKS, delta, 0)
+        lax.fori_loop(0, CHUNKS, delta, 0, unroll=2)
         saw = jnp.broadcast_to(seen[o], (HEADS, TEXT)) > 0.0
         stats[j, slot_of(o), 0] = jnp.where(saw, w_ref[o], NEGATIVE)
         stats[j, slot_of(o), 1] = jnp.where(saw, d_ref[o], 0.0)
@@ -444,28 +438,14 @@
         )
     for c in swaps:
         c.start()
-    for step in range(1, GROUP):
-        other = (j + step) % GROUP
-        remote(stats.at[j], stats.at[other], stat_send.at[0], stat_recv.at[other], near).wait_recv()
-
-    gate_sum = jnp.zeros((HEADS, TEXT), F32)
+
+    saws = [jnp.broadcast_to(seen[o], (HEADS, TEXT)) > 0.0 for o in range(2)]
+    mine_lse = [jnp.where(saws[o], w_ref[o], NEGATIVE) for o in range(2)]
+    peak = jnp.maximum(mine_lse[0], mine_lse[1])
+    shares = [jnp.exp(x - peak) for x in mine_lse]
     for o in range(2):
-        mine = [img_ref[2 * base + i] - base == docs[o] for i in range(2 * GROUP)]
-        lses = [
-            jnp.where(mine[i], stats[i // 2, i % 2, 0], 2.0 * NEGATIVE) for i in range(2 * GROUP)
-        ]
-        top = functools.reduce(jnp.maximum, lses)
-        terms = [jnp.exp(x - top) for x in lses]
-        total = functools.reduce(jnp.add, terms)
-        weighted = [
-            t * jnp.where(mine[i], stats[i // 2, i % 2, 1], 0.0) for i, t in enumerate(terms)
-        ]
-        saw = jnp.broadcast_to(seen[o], (HEADS, TEXT)) > 0.0
-        own = jnp.where(saw, w_ref[o], NEGATIVE)
-        d_ref[o] = functools.reduce(jnp.add, weighted) / total
-        f_ref[o] = jnp.where(saw, jnp.exp(m_ref[o] - (top + jnp.log(total))), 0.0)
-        w_ref[o] = jnp.where(saw, jnp.exp(own - top) / total, 0.0)
-        gate_sum = gate_sum + w_ref[o] * gam_ref[o]
+        local = jnp.where(rels[0] == rels[1], shares[o] / (shares[0] + shares[1]), 1.0)
+        lw_ref[o] = jnp.where(saws[o], local, 0.0)
 
     def share(pair, own_b, near_b, far_b, k, lanes):
         def total(r):
@@ -521,18 +501,52 @@
             hc = k * (PER // 2) + c
             pair = []
             for o in range(2):
-                w = [w_ref[o, pl.ds(2 * hc + h, 1), :] for h in range(2)]
+                w = [lw_ref[o, pl.ds(2 * hc + h, 1), :] for h in range(2)]
                 x = o_ref[o, k, :, pl.ds(pl.multiple_of(c * ROWS, ROWS), ROWS)]
                 x = x * jnp.concatenate(w, axis=1)
                 pair.append(jnp.concatenate([x[:, :TEXT].T, x[:, TEXT:].T], axis=1))
             share(pair, own_o, near_o, far_o, k, pl.ds(pl.multiple_of(c * ROWS, ROWS), ROWS))
             return carry
 
-        lax.fori_loop(0, PER // 2, body, 0)
+        lax.fori_loop(0, PER // 2, body, 0, unroll=2)
         start_returns(0, k, *o_args)
         return carry
 
     lax.fori_loop(0, KV, give_out, 0)
+
+    for step in range(1, GROUP):
+        other = (j + step) % GROUP
+        remote(stats.at[j], stats.at[other], stat_send.at[0], stat_recv.at[other], near).wait_recv()
+
+    def of_document(doc):
+        mine = [img_ref[2 * base + i] - base == doc for i in range(2 * GROUP)]
+        lses = [
+            jnp.where(mine[i], stats[i // 2, i % 2, 0], 2.0 * NEGATIVE) for i in range(2 * GROUP)
+        ]
+        top = functools.reduce(jnp.maximum, lses)
+        terms = [jnp.exp(x - top) for x in lses]
+        return mine, top, terms, functools.reduce(jnp.add, terms)
+
+    _, _, terms, total = of_document(j)
+    for r, holder in enumerate((j, near - base, far - base)):
+        weight = jnp.zeros((HEADS, TEXT), F32)
+        for i in range(2 * GROUP):
+            weight = weight + jnp.where(holder == i // 2, terms[i], 0.0)
+        fill = jnp.zeros((DIM - HEADS, TEXT), F32)
+        wt_ref[r] = jnp.concatenate([weight / total, fill], axis=0).T
+
+    gate_sum = jnp.zeros((HEADS, TEXT), F32)
+    for o in range(2):
+        mine, top, terms, total = of_document(docs[o])
+        weighted = [
+            t * jnp.where(mine[i], stats[i // 2, i % 2, 1], 0.0) for i, t in enumerate(terms)
+        ]
+        saw = jnp.broadcast_to(seen[o], (HEADS, TEXT)) > 0.0
+        own = jnp.where(saw, w_ref[o], NEGATIVE)
+        d_ref[o] = functools.reduce(jnp.add, weighted) / total
+        f_ref[o] = jnp.where(saw, jnp.exp(m_ref[o] - (top + jnp.log(total))), 0.0)
+        w_ref[o] = jnp.where(saw, jnp.exp(own - top) / total, 0.0)
+        gate_sum = gate_sum + w_ref[o] * gam_ref[o]
 
     def backward(k, sums):
         kgain_sum, qgain_sum = sums
@@ -545,8 +559,8 @@
                 dp = dot(vpad[o, k, a : a + n, :], gsT[o, k])
                 p = e_ref[2 * o + k, a : a + n, :] * factor
                 ds = (p * (dp - delta)).astype(BF16)
-                value = dot(p.astype(BF16), gs[o, k])
-                e_ref[2 * o + k, a : a + n, :DIM] = dot(ds, qh[o, k])
+                value = crossed(gsT[o, k], p.astype(BF16)).T
+                e_ref[2 * o + k, a : a + n, :DIM] = crossed(qhT[o, k], ds).T
                 if n < 2 * DIM:
                     ds = jnp.concatenate([ds, jnp.zeros((DEEP - a - n, SPAN), BF16)], axis=0)
                 part = dot(turned_k[o, k, :, a : a + ds.shape[0]], ds)
@@ -578,7 +592,7 @@
                     qgain_sum = qgain_sum + fold(pair[o][:, part] * unit, jnp.sum)
             return qgain_sum
 
-        qgain_sum = lax.fori_loop(0, PER // 2, body, qgain_sum)
+        qgain_sum = lax.fori_loop(0, PER // 2, body, qgain_sum, unroll=2)
         start_returns(1, k, *q_args)
 
         def norm_back(o, kgain_sum):
@@ -662,15 +676,13 @@
     for k in range(KV):
         wait_returns(0, k, *o_args)
 
-    def attend(k, carry):
-        for c in range(PER):
-            lanes = slice(c * DIM, (c + 1) * DIM)
-            full = pl.ds(pl.multiple_of(k * PER * DIM + c * DIM, DIM), DIM)
-            merged = own_o[k, :, lanes] + rnear_o[k, :, lanes] + rfar_o[k, :, lanes].astype(F32)
-            gbuf[0, :, full] = (gate * merged).astype(BF16)
-        return carry
-
-    lax.fori_loop(0, KV, attend, 0)
+    for h in range(HEADS):
+        k, lanes = h // PER, slice(h % PER * DIM, (h % PER + 1) * DIM)
+        parts = (own_o[k, :, lanes], rnear_o[k, :, lanes], rfar_o[k, :, lanes].astype(F32))
+        merged = functools.reduce(
+            jnp.add, [wt_ref[r, :, h : h + 1] * x for r, x in enumerate(parts)]
+        )
+        gbuf[0, :, h * DIM : (h + 1) * DIM] = (gate * merged).astype(BF16)
     out_att = pltpu.make_async_copy(gbuf.at[0], att_hbm.at[0], out_sem.at[4])
     out_att.start()
     if len(stages) > 1:
@@ -705,7 +717,7 @@
     for n in range(len(stages)):
         for c in stage_copies(n)[0]:
             c.wait_send()
-    for c in (*q_near, g_near, g_far):
+    for c in (*q_near, *q_far, g_near, g_far):
         c.wait_send()
     for c in swaps:
         c.wait_send()
@@ -748,6 +760,8 @@
         vm((2, HEADS, TEXT), F32),
         vm((2, HEADS, TEXT), F32),
         vm((2, HEADS, TEXT), F32),
+        vm((2, HEADS, TEXT), F32),
+        vm((3, TEXT, DIM), F32),
         vm((GROUP, 2, 2, HEADS, TEXT), F32),
         vm(half, F32),
         vm(half, F32),

time: 84.4 us -> 80.6 us (0.955)
  Pallas kernels: 83 us -> 79.2 us
    pallas_call x1, Pallas kernels: 78.3 us -> 74.5 us  [run_main(): pl.pallas_call(functools.partial(main_kernel, stages), out_shape=(jax.Sha...]
where the time goes in v4:
time: 80.6 us; the launch traced here: 80.5 us
  Pallas kernels  79.2 us (98%)
  between operations  1.29 us (2%)
    pallas_call x1, Pallas kernels, run_main(): pl.pallas_call(functools.partial(main_kernel, stages), out_shape=(jax.Sha...  74.5 us
    pallas_call x1, Pallas kernels, settled(): pl.pallas_call(functools.partial(copy_kernel, count), out_shape=tuple((ja...  4.7 us

profile of v4, /device:TPU:1, one launch (start us, length us, event | category | flops | bytes accessed | tf_op | source)
XLA Modules:
  0.0 80.5 jit_solution(12468440581796818860)
XLA Ops:
  1.3 74.5 %shard_map.144 = (bf16[1,128,2048]{2,1,0:T(8,128)(2,1)}, bf16[1,128,2048]{2,1,0:T(8,128)(2,1)}, bf16[1601,4,128]{2,1,0:T(4,128)(2,1)}, bf16[1601,4,128]{2,1,0:T(...) custom-call(s32[128]{0:T(128)} %img_ref.1, f32[1,1]{1,0:T(1,128)} %bitcast.31.gate_ref, ...), custom_call_target="tpu_custom_call" | custom-call | tf_op jit(solution)/shard_map/pallas_call | solution.py:789
  75.8 4.7 %shard_map.145 = (bf16[1,128,2048]{2,1,0:T(8,128)(2,1)}, bf16[1,128,2048]{2,1,0:T(8,128)(2,1)}, bf16[1601,4,128]{2,1,0:T(4,128)(2,1)}, bf16[1601,4,128]{2,1,0:T(...) custom-call(bf16[1,128,2048]{2,1,0:T(8,128)(2,1)} %get-tuple-element.21.refs_0_, ...), custom_call_target="tpu_custom_call" | custom-call | tf_op jit(solution)/shard_map/pallas_call | solution.py:849

commit v5 on v4

--- a/solution.py
+++ b/solution.py
@@ -447,15 +447,17 @@
         local = jnp.where(rels[0] == rels[1], shares[o] / (shares[0] + shares[1]), 1.0)
         lw_ref[o] = jnp.where(saws[o], local, 0.0)
 
-    def share(pair, own_b, near_b, far_b, k, lanes):
-        def total(r):
-            a = jnp.where(rels[0] == r, pair[0], 0.0)
-            return a + jnp.where(rels[1] == r, pair[1], 0.0)
-
-        own_b[k, :, lanes] = total(0)
-        near_b[k, :, lanes] = total(1)
-        far_b[0, k, :, lanes] = total(2).astype(BF16)
-        far_b[1, k, :, lanes] = total(3).astype(BF16)
+    def total_of(pair, r):
+        a = jnp.where(rels[0] == r, pair[0], 0.0)
+        return a + jnp.where(rels[1] == r, pair[1], 0.0)
+
+    def share_far(pair, far_b, k, lanes):
+        far_b[0, k, :, lanes] = total_of(pair, 2).astype(BF16)
+        far_b[1, k, :, lanes] = total_of(pair, 3).astype(BF16)
+
+    def share_near(pair, own_b, near_b, k, lanes):
+        own_b[k, :, lanes] = total_of(pair, 0)
+        near_b[k, :, lanes] = total_of(pair, 1)
 
     def returns(which, k, near_b, far_b, rnear_b, rfar_b):
         one = remote(
@@ -470,14 +472,11 @@
         ]
         return one, two
 
-    def start_returns(*args):
-        one, two = returns(*args)
-        one.start()
-
-        @pl.when(inner)
-        def _():
-            for c in two:
-                c.start()
+    def start_far(*args):
+        start_where(inner, *returns(*args)[1])
+
+    def start_near(*args):
+        returns(*args)[0].start()
 
     def finish_sends(*args):
         one, two = returns(*args)
@@ -505,11 +504,14 @@
                 x = o_ref[o, k, :, pl.ds(pl.multiple_of(c * ROWS, ROWS), ROWS)]
                 x = x * jnp.concatenate(w, axis=1)
                 pair.append(jnp.concatenate([x[:, :TEXT].T, x[:, TEXT:].T], axis=1))
-            share(pair, own_o, near_o, far_o, k, pl.ds(pl.multiple_of(c * ROWS, ROWS), ROWS))
+            lanes = pl.ds(pl.multiple_of(c * ROWS, ROWS), ROWS)
+            share_far(pair, far_o, k, lanes)
+            share_near(pair, own_o, near_o, k, lanes)
             return carry
 
         lax.fori_loop(0, PER // 2, body, 0, unroll=2)
-        start_returns(0, k, *o_args)
+        start_far(0, k, *o_args)
+        start_near(0, k, *o_args)
         return carry
 
     lax.fori_loop(0, KV, give_out, 0)
@@ -580,9 +582,17 @@
 
         lax.fori_loop(0, 2, per_slot, 0)
 
+        def give_far(c, carry):
+            lanes = pl.ds(pl.multiple_of(c * ROWS, ROWS), ROWS)
+            share_far([dq_ref[0, c], dq_ref[1, c]], far_q, k, lanes)
+            return carry
+
+        lax.fori_loop(0, PER // 2, give_far, 0, unroll=2)
+        start_far(1, k, *q_args)
+
         def body(c, qgain_sum):
             pair = [dq_ref[0, c], dq_ref[1, c]]
-            share(pair, own_q, near_q, far_q, k, pl.ds(pl.multiple_of(c * ROWS, ROWS), ROWS))
+            share_near(pair, own_q, near_q, k, pl.ds(pl.multiple_of(c * ROWS, ROWS), ROWS))
             full = pl.ds(pl.multiple_of(k * PER * DIM + c * ROWS, ROWS), ROWS)
             for o in range(2):
                 x = chosen(qbuf, o, 3 + o, full)
@@ -593,7 +603,7 @@
             return qgain_sum
 
         qgain_sum = lax.fori_loop(0, PER // 2, body, qgain_sum, unroll=2)
-        start_returns(1, k, *q_args)
+        start_near(1, k, *q_args)
 
         def norm_back(o, kgain_sum):
             def key_step(x, up, kgain_sum):

time: 80.6 us -> 80 us (level)
  no operation moved by 1% of the time
where the time goes in v5:
time: 80 us; the launch traced here: 79.8 us
  Pallas kernels  78.6 us (98%)
  between operations  1.29 us (2%)
    pallas_call x1, Pallas kernels, run_main(): pl.pallas_call(functools.partial(main_kernel, stages), out_shape=(jax.Sha...  73.9 us
    pallas_call x1, Pallas kernels, settled(): pl.pallas_call(functools.partial(copy_kernel, count), out_shape=tuple((ja...  4.7 us

profile of v5, /device:TPU:1, one launch (start us, length us, event | category | flops | bytes accessed | tf_op | source)
XLA Modules:
  0.0 79.8 jit_solution(17350762005967829105)
XLA Ops:
  1.3 73.9 %shard_map.144 = (bf16[1,128,2048]{2,1,0:T(8,128)(2,1)}, bf16[1,128,2048]{2,1,0:T(8,128)(2,1)}, bf16[1601,4,128]{2,1,0:T(4,128)(2,1)}, bf16[1601,4,128]{2,1,0:T(...) custom-call(s32[128]{0:T(128)} %img_ref.1, f32[1,1]{1,0:T(1,128)} %bitcast.31.gate_ref, ...), custom_call_target="tpu_custom_call" | custom-call | tf_op jit(solution)/shard_map/pallas_call | solution.py:799
  75.1 4.7 %shard_map.145 = (bf16[1,128,2048]{2,1,0:T(8,128)(2,1)}, bf16[1,128,2048]{2,1,0:T(8,128)(2,1)}, bf16[1601,4,128]{2,1,0:T(4,128)(2,1)}, bf16[1601,4,128]{2,1,0:T(...) custom-call(bf16[1,128,2048]{2,1,0:T(8,128)(2,1)} %get-tuple-element.21.refs_0_, ...), custom_call_target="tpu_custom_call" | custom-call | tf_op jit(solution)/shard_map/pallas_call | solution.py:859
